TPU v7x, 256 devices: a whole 4x4x8 slice. The times are simulated.
256 devices in a mesh: ty: 16 (over z_lo, x, core), tx: 16 (over z_hi, y).
Axes of the slice: x: 4, y: 4, z: 8 (z_hi: 4, z_lo: 2; z = z_hi * 2 + z_lo), core: 2. Of those that a mesh axis runs over, the one named last changes fastest.
Arguments:
- sky_tile: bfloat16 [6, 2048, 4096], P(None, 'ty', 'tx'), may hold values from -6 to 6
- request_offset: int32 [16, 16, 8, 2, 2], P('ty', 'tx'), may hold values from 0 to 192, as said below
- request_count: int32 [16, 16, 8], P('ty', 'tx'), may hold values from 0 to 2, as said below
- tile_target: float32 [16, 16, 8, 512], P('ty', 'tx'), may hold values from -6 to 6
- cut_target: float32 [16, 16, 8, 1024], P('ty', 'tx'), may hold values from -6 to 6
- w_first: bfloat16 [24, 64], replicated, may hold values from -1.25 to 1.25
- w_second: bfloat16 [256, 128], replicated, may hold values from -0.375 to 0.375
- w_third: bfloat16 [512, 256], replicated, may hold values from -0.25 to 0.25
- w_head: bfloat16 [8, 256], replicated, may hold values from -0.375 to 0.375
Outputs:
- grad_first: float32 [24, 64], replicated
- grad_second: float32 [256, 128], replicated
- grad_third: float32 [512, 256], replicated
- grad_head: float32 [8, 256], replicated
- cut_pred: bfloat16 [16, 16, 8, 1024], P('ty', 'tx')
Inputs may be any that keep to these rules, and one draw needn't show every extreme that they name: request_count[r, c, k] of the 2 slots of direction k are used; it is zero where that neighbour lies outside the grid, and some tile uses all 2 slots of all eight directions. `request_offset`: offsets are in the frame of the neighbouring tile; every cutout lies within 96 pixels of the border that this neighbour shares with tile (r, c) along each axis where the direction moves.
All inputs are finite; a program needn't handle non-finite values.
Results may differ from a plain program's by a relative error of at most 0.002.
The roundings to bfloat16 on the way count: a program that leaves them out, or rounds other values in their place, can miss the bound.
Values may be sent and summed in bfloat16 or wider, within the bound.
A program may use at most 128 MiB of HBM per device.

v0:
```python
import jax
import jax.numpy as jnp
from jax import lax
from jax.sharding import PartitionSpec as P

CUT = 64


DIRECTIONS = ((-1, -1), (-1, 0), (-1, 1), (0, -1), (0, 1), (1, -1), (1, 0), (1, 1))


def shifted(block, axis, distance):
    devices = range(lax.axis_size(axis))
    route = [(i - distance, i) for i in devices if i - distance in devices]
    return lax.ppermute(block, axis, route)


def inner(left_mat, right_mat):
    return lax.dot_general(
        left_mat, right_mat, (((0,), (0,)), ((), ())), preferred_element_type=jnp.float32
    )


def outer(left_mat, right_mat):
    return lax.dot_general(
        left_mat, right_mat, (((1,), (1,)), ((), ())), preferred_element_type=jnp.float32
    )


def patchify(field_now):
    channels, batch_size, rows_in, cols_in = field_now.shape
    blocks = field_now.reshape(channels, batch_size, rows_in // 2, 2, cols_in // 2, 2)
    blocks = blocks.transpose(0, 3, 5, 1, 2, 4)
    return blocks.reshape(channels * 4, batch_size * (rows_in // 2) * (cols_in // 2))


def unpatchify(grads_in, shape_in):
    channels, batch_size, rows_in, cols_in = shape_in
    blocks = grads_in.reshape(channels, 2, 2, batch_size, rows_in // 2, cols_in // 2)
    blocks = blocks.transpose(0, 3, 4, 1, 5, 2)
    return blocks.reshape(channels, batch_size * rows_in * cols_in)


def activation_slope(pre_act):
    sigmoid_value = jax.nn.sigmoid(pre_act)
    return sigmoid_value * (1.0 + pre_act * (1.0 - sigmoid_value))


def forward(image_stack, weights):
    stored = []
    field_now = image_stack
    active = image_stack
    for weight_matrix in weights[:3]:
        shape_in = field_now.shape
        patches = patchify(field_now)
        pre_act = inner(weight_matrix, patches)
        active = jax.nn.silu(pre_act).astype(jnp.bfloat16)
        stored.append((patches, pre_act, shape_in))
        field_now = active.reshape(
            weight_matrix.shape[1], shape_in[1], shape_in[2] // 2, shape_in[3] // 2
        )
    predicted = jnp.dot(weights[3], active, preferred_element_type=jnp.float32)
    return (stored, active, predicted)


def add_terms(term_list):
    running_total = term_list[0]
    for extra_term in term_list[1:]:
        running_total = running_total + extra_term
    return running_total


def backward(path_list, weights, finish):
    results = [None, None, None, None]
    results[3] = finish(
        add_terms([outer(loss_grad, top_act) for stored, top_act, loss_grad in path_list])
    )
    deltas = []
    for stored, top_act, loss_grad in path_list:
        upward = inner(weights[3], loss_grad)
        deltas.append((upward * activation_slope(stored[2][1])).astype(jnp.bfloat16))
    for layer_index in (2, 1, 0):
        term_list = [
            outer(path_item[0][layer_index][0], delta_now)
            for path_item, delta_now in zip(path_list, deltas)
        ]
        results[layer_index] = finish(add_terms(term_list))
        if layer_index > 0:
            fresh_deltas = []
            for path_item, delta_now in zip(path_list, deltas):
                upward = jnp.dot(
                    weights[layer_index], delta_now, preferred_element_type=jnp.float32
                )
                upward = unpatchify(upward, path_item[0][layer_index][2])
                fresh_deltas.append(
                    (upward * activation_slope(path_item[0][layer_index - 1][1])).astype(
                        jnp.bfloat16
                    )
                )
            deltas = fresh_deltas
    return tuple(results)


def unchanged(summed_term):
    return summed_term


def cut_from(source_image, rows_at, cols_at):
    band_count = source_image.shape[0]
    zero_index = jnp.zeros((), jnp.int32)

    def window(row_at, col_at):
        return lax.dynamic_slice(
            source_image, (zero_index, row_at, col_at), (band_count, CUT, CUT)
        ).reshape(band_count, CUT * CUT)

    flattened = jax.vmap(window)(rows_at.reshape(-1), cols_at.reshape(-1))
    return flattened.reshape(rows_at.shape + (band_count, CUT * CUT))


def slot_mask(counts, slot_count, positions):
    valid_slots = (
        (jnp.arange(slot_count, dtype=jnp.int32)[None, :] < counts[:, None])
        .astype(jnp.float32)
        .reshape(-1)
    )
    return jnp.repeat(valid_slots, positions)


def request_rows(payload, step_by):
    return shifted(payload, "ty", step_by)


def request_cols(payload, step_by):
    return shifted(payload, "tx", step_by)


def reply_rows(payload, step_by):
    return shifted(payload, "ty", step_by)


def reply_cols(payload, step_by):
    return shifted(payload, "tx", step_by)


def per_device(
    sky_tile,
    request_offset,
    request_count,
    tile_target,
    cut_target,
    w_first,
    w_second,
    w_third,
    w_head,
):
    weights = (w_first, w_second, w_third, w_head)
    band_count, tile_height, tile_width = sky_tile.shape
    tile_total = lax.axis_size("ty") * lax.axis_size("tx")
    offsets = request_offset[0, 0]
    counts = request_count[0, 0]
    slot_count = offsets.shape[-1]
    own_stored, own_top, own_pred = forward(sky_tile[:, None], weights)
    own_grad = ((own_pred - tile_target[0, 0]) / tile_total).astype(jnp.bfloat16)
    arrived = []
    for slot_index, (step_y, step_x) in enumerate(DIRECTIONS):
        moved_part = offsets[slot_index]
        if step_y != 0:
            moved_part = request_rows(moved_part, step_y)
        if step_x != 0:
            moved_part = request_cols(moved_part, step_x)
        arrived.append(moved_part)
    wanted = jnp.stack(arrived)
    pieces = cut_from(sky_tile, wanted[:, 0], wanted[:, 1])
    returned = []
    for slot_index, (step_y, step_x) in enumerate(DIRECTIONS):
        piece_now = pieces[slot_index]
        if step_x != 0:
            piece_now = reply_cols(piece_now, -step_x)
        if step_y != 0:
            piece_now = reply_rows(piece_now, -step_y)
        returned.append(piece_now)
    received = jnp.stack(returned)
    net_input = received.reshape(8 * slot_count, band_count, CUT, CUT).transpose(1, 0, 2, 3)
    cut_stored, cut_top, cut_full = forward(net_input, weights)
    mask_full = slot_mask(counts, slot_count, cut_full.shape[1] // (8 * slot_count))
    cut_grad = ((cut_full - cut_target[0, 0]) * mask_full / tile_total).astype(jnp.bfloat16)
    cut_flat = (cut_full * mask_full).astype(jnp.bfloat16)
    path_list = [(own_stored, own_top, own_grad), (cut_stored, cut_top, cut_grad)]
    local_grads = backward(path_list, weights, unchanged)
    summed = lax.psum(
        (local_grads[0], local_grads[1], local_grads[2], local_grads[3]), ("ty", "tx")
    )
    cut_pred = cut_flat[None, None]
    return (summed[0], summed[1], summed[2], summed[3], cut_pred)


def solution(mesh):
    return jax.shard_map(
        per_device,
        mesh=mesh,
        in_specs=(
            P(None, "ty", "tx"),
            P("ty", "tx", None, None, None),
            P("ty", "tx", None),
            P("ty", "tx", None, None),
            P("ty", "tx", None, None),
            P(),
            P(),
            P(),
            P(),
        ),
        out_specs=(P(), P(), P(), P(), P("ty", "tx", None, None)),
        check_vma=False,
    )
```

profile of v0, /device:TPU:1, one launch (start us, length us, event | category | flops | bytes accessed | tf_op | source)
XLA Modules:
  0.0 775.3 jit_solution(6475510810300099900)
XLA Ops:
  9.2 5.1 collective-permute-start
  16.3 3.6 collective-permute-start.7
  21.9 2.9 collective-permute-start.2
  24.8 7.4 copy.47
  32.2 12.0 %copy.48 = bf16[6,2,2,1,64,128]{5,4,2,1,0,3:T(8,128)(2,1)S(1)} copy(bf16[6,2,2,1,64,128]{0,2,5,1,4,3:T(2,128)(2,1)} %bitcast.208) | data formatting | bytes 786432 | tf_op jit(solution)/shard_map/transpose | solution.py:33
  44.2 2.2 multiply_convert_fusion.5
  47.5 4.4 copy.50
  51.9 3.4 reshape.156
  57.0 3.5 copy.51
  60.5 2.8 reshape.157
  66.7 2.5 reshape.158
  69.3 3.9 copy.53
  77.9 2.4 collective-permute-done.5
  82.6 4.4 collective-permute-start.9
  89.1 4.5 collective-permute-start.4
  95.0 5.9 collective-permute-start.11
  102.2 47.7 %while.1 = (s32[]{:T(128)}, bf16[6,128,256]{2,1,0:T(8,128)(2,1)}, s32[16,3]{0,1:T(4,128)S(1)}, bf16[16,6,64,64]{3,2,1,0:T(8,128)(2,1)S(1)}, s32[]{:T(128)}) while((s32[]{:T(128)}, bf16[6,128,256]{2,1,0:T(8,128)(2,1)}, s32[16,3]{0,1:T(4,128)S(1)}, bf16[16,6,64,64]{3,2,1,0:T(8,128)(2,1)S(1)}, s32[]{:T(128)}) %tuple.53), condition=%wide.while_cond, body=%wide.while_body.sunk | while | flops 2 | bytes 147573 | solution.py:113
  102.8 2.4 bitcast_dynamic-update-slice_fusion.10
  105.8 2.4 bitcast_dynamic-update-slice_fusion.10
  108.7 2.4 bitcast_dynamic-update-slice_fusion.10
  111.7 2.4 bitcast_dynamic-update-slice_fusion.10
  114.7 2.4 bitcast_dynamic-update-slice_fusion.10
  117.7 2.4 bitcast_dynamic-update-slice_fusion.10
  120.7 2.4 bitcast_dynamic-update-slice_fusion.10
  123.6 2.4 bitcast_dynamic-update-slice_fusion.10
  126.6 2.4 bitcast_dynamic-update-slice_fusion.10
  129.6 2.4 bitcast_dynamic-update-slice_fusion.10
  132.6 2.4 bitcast_dynamic-update-slice_fusion.10
  135.6 2.4 bitcast_dynamic-update-slice_fusion.10
  138.5 2.4 bitcast_dynamic-update-slice_fusion.10
  141.5 2.4 bitcast_dynamic-update-slice_fusion.10
  144.5 2.4 bitcast_dynamic-update-slice_fusion.10
  147.5 2.4 bitcast_dynamic-update-slice_fusion.10
  152.2 4.6 collective-permute-start.12
  158.7 17.4 %collective-permute-start.13 = (bf16[2,6,4096]{2,0,1:T(2,128)(2,1)}, bf16[2,6,4096]{2,0,1:T(2,128)(2,1)S(1)}, u32[]{:S(2)}, u32[]{:S(2)}) collective-permute-start(bf16[2,6,4096]{2,0,1:T(2,128)(2,1)} %collective-permute-done.12), channel_id=1, source_target_pairs={{0,16},{16,32},{32,48},{48,64},{64,80},{80,96},{96,112},{112,128},... | collective-permute-start | bytes 294920 | tf_op jit(solution)/shard_map/ppermute | solution.py:15
  178.3 3.1 reshape.160
  181.4 7.5 copy.55
  188.9 3.9 copy.56
  197.0 7.4 collective-permute-start.17
  206.8 7.2 collective-permute-start.19
  215.5 4.0 collective-permute-start.16
  223.1 3.8 collective-permute-start.20
  230.4 2.5 collective-permute-done.23
  234.7 4.7 copy.76
  239.4 14.8 %copy.77 = bf16[6,2,2,16,32,32]{5,4,3,2,1,0:T(8,128)(2,1)S(1)} copy(bf16[6,2,2,16,32,32]{3,2,5,1,4,0:T(2,128)(2,1)} %bitcast.209) | data formatting | bytes 1572864 | tf_op jit(solution)/shard_map/transpose | solution.py:33
  254.2 4.1 reshape.164
  258.3 4.5 multiply_convert_fusion.1
  262.9 3.1 copy.78
  266.0 23.1 %copy.79 = bf16[64,2,2,16,16,16]{5,4,3,2,1,0:T(8,128)(2,1)} copy(bf16[64,2,2,16,16,16]{0,2,5,1,4,3:T(2,128)(2,1)} %bitcast.211) | data formatting | bytes 4194304 | tf_op jit(solution)/shard_map/transpose | solution.py:33
  289.2 29.0 %reshape.165 = bf16[256,4096]{1,0:T(8,128)(2,1)S(1)} reshape(bf16[64,2,2,16,16,16]{5,4,3,2,1,0:T(8,128)(2,1)} %copy.79) | data formatting | bytes 4194304 | tf_op jit(solution)/shard_map/reshape | solution.py:34
  318.2 3.2 multiply_convert_fusion.3
  321.4 22.6 %copy.80 = bf16[128,16,8,2,8,2]{4,2,1,5,3,0:T(8,128)(2,1)} copy(bf16[128,16,8,2,8,2]{0,5,4,3,2,1:T(2,128)(2,1)S(1)} %bitcast.219) | data formatting | bytes 2097152 | tf_op jit(solution)/shard_map/reshape;reshape | solution.py:32
  344.0 24.5 %reshape.166 = bf16[512,1024]{1,0:T(8,128)(2,1)S(1)} reshape(bf16[128,2,2,16,8,8]{5,4,3,2,1,0:T(8,128)(2,1)} %bitcast.206) | data formatting | bytes 2097152 | tf_op jit(solution)/shard_map/reshape | solution.py:34
  375.6 21.4 %reshape.167 = f32[128,2,2,16,8,8]{5,4,3,2,1,0:T(8,128)} reshape(f32[512,1024]{1,0:T(8,128)S(1)} %copy.81) | data formatting | bytes 4194304 | tf_op jit(solution)/shard_map/reshape | solution.py:39
  397.0 23.0 %copy.82 = f32[128,16,8,2,8,2]{0,5,4,3,2,1:T(2,128)S(1)} copy(f32[128,16,8,2,8,2]{4,2,1,5,3,0:T(8,128)} %bitcast.205) | data formatting | bytes 4194304 | tf_op jit(solution)/shard_map/transpose | solution.py:40
  420.0 2.4 multiply_convert_fusion.2
  422.5 2.7 convolution_bitcast_fusion.1
  426.5 5.7 copy.83
  432.2 19.0 %reshape.169 = f32[64,2,2,16,16,16]{5,4,3,2,1,0:T(8,128)} reshape(f32[256,4096]{1,0:T(8,128)} %copy.83) | data formatting | bytes 8388608 | tf_op jit(solution)/shard_map/reshape | solution.py:39
  451.2 27.3 %copy.84 = f32[64,16,16,2,16,2]{0,5,4,3,2,1:T(2,128)} copy(f32[64,16,16,2,16,2]{4,2,1,5,3,0:T(8,128)} %bitcast.204) | data formatting | bytes 8388608 | tf_op jit(solution)/shard_map/transpose | solution.py:40
  478.5 6.9 copy.85
  485.4 5.2 fusion
  492.1 104.9 %all-reduce = (f32[24,64]{1,0:T(8,128)}, f32[8,256]{1,0:T(8,128)}) all-reduce(f32[24,64]{1,0:T(8,128)S(1)} %fusion.7, f32[8,256]{1,0:T(8,128)S(1)} %convolution_add_fusion.2), channel_id=1, replica_groups=mesh['ty'=16,'tx'=16] {'ty','tx'}, use_global_device_ids=true, to_apply=%region_0.1 | all-reduce | flops 3584 | bytes 28672 | tf_op jit(solution)/shard_map/psum | solution.py:191
  597.0 167.7 %all-reduce.4.cloned.1.call-done = (f32[256,128]{1,0:T(8,128)}, f32[512,256]{1,0:T(8,128)}) async-done(((f32[256,128]{1,0:T(8,128)}, f32[512,256]{1,0:T(8,128)}), (f32[256,128]{1,0:T(8,128)}, f32[512,256]{1,0:T(8,128)})) %all-reduce.4.cloned.1.call-update) | async-done | bytes 655376 | tf_op jit(solution)/shard_map/psum | solution.py:191
  (204 shorter events, 69.7 us)
Async XLA Ops:
  7.2 56.1 %copy-start = (bf16[512,256]{1,0:T(8,128)(2,1)S(1)}, bf16[512,256]{1,0:T(8,128)(2,1)}, u32[]{:S(2)}) copy-start(bf16[512,256]{1,0:T(8,128)(2,1)} %param.16) | copy-start | bytes 786436
  7.2 757.5 %all-reduce.4.cloned.1.call-start = ((), (), s32[]{:S(2)}) async-start(), calls=%async_computation | async-start | bytes 1310720 | tf_op jit(solution)/shard_map/psum | solution.py:191
  9.2 78.6 %collective-permute-start = (s32[2,2]{1,0:T(2,128)}, s32[2,2]{1,0:T(2,128)}, u32[]{:S(2)}, u32[]{:S(2)}) collective-permute-start(s32[2,2]{1,0:T(2,128)} %get-tuple-element.19), channel_id=1, source_target_pairs={{16,0},{32,16},{48,32},{64,48},{80,64},{96,80},{112,96},{128,112},... | collective-permute-start | bytes 56 | tf_op jit(solution)/shard_map/ppermute | solution.py:15
  14.4 74.7 %collective-permute-start.3 = (s32[2,2]{1,0:T(2,128)}, s32[2,2]{1,0:T(2,128)}, u32[]{:S(2)}, u32[]{:S(2)}) collective-permute-start(s32[2,2]{1,0:T(2,128)} %get-tuple-element.17), channel_id=1, source_target_pairs={{16,0},{32,16},{48,32},{64,48},{80,64},{96,80},{112,96},{128,112},... | collective-permute-start | bytes 56 | tf_op jit(solution)/shard_map/ppermute | solution.py:15
  16.3 77.3 %collective-permute-start.7 = (s32[2,2]{1,0:T(2,128)}, s32[2,2]{1,0:T(2,128)}, u32[]{:S(2)}, u32[]{:S(2)}) collective-permute-start(s32[2,2]{1,0:T(2,128)} %get-tuple-element.14), channel_id=1, source_target_pairs={{0,16},{16,32},{32,48},{48,64},{64,80},{80,96},{96,112},{112,128},... | collective-permute-start | bytes 56 | tf_op jit(solution)/shard_map/ppermute | solution.py:15
  20.0 75.0 %collective-permute-start.10 = (s32[2,2]{1,0:T(2,128)S(1)}, s32[2,2]{1,0:T(2,128)}, u32[]{:S(2)}, u32[]{:S(2)}) collective-permute-start(s32[2,2]{1,0:T(2,128)S(1)} %get-tuple-element.13), channel_id=1, source_target_pairs={{0,16},{16,32},{32,48},{48,64},{64,80},{80,96},{96,112},{112,128},... | collective-permute-start | bytes 56 | tf_op jit(solution)/shard_map/ppermute | solution.py:15
  21.9 54.0 %collective-permute-start.2 = (s32[2,2]{1,0:T(2,128)}, s32[2,2]{1,0:T(2,128)}, u32[]{:S(2)}, u32[]{:S(2)}) collective-permute-start(s32[2,2]{1,0:T(2,128)} %get-tuple-element.18), channel_id=1, source_target_pairs={{16,0},{32,16},{48,32},{64,48},{80,64},{96,80},{112,96},{128,112},... | collective-permute-start | bytes 56 | tf_op jit(solution)/shard_map/ppermute | solution.py:15
  32.2 12.0 %copy-start.29 = (bf16[24,64]{1,0:T(8,128)(2,1)S(1)}, bf16[24,64]{1,0:T(8,128)(2,1)}, u32[]{:S(2)}) copy-start(bf16[24,64]{1,0:T(8,128)(2,1)} %param.14) | copy-start | bytes 9220
  44.2 2.2 copy-start.17
  51.9 3.4 copy-start.19
  63.2 1.4 copy-start.23
  63.2 1.4 copy-start.24
  64.7 0.7 copy-start.9
  65.4 0.7 copy-start.11
  69.3 3.9 copy-start.8
  73.2 0.9 copy-start.20
  73.6 2.3 copy-start.27
  73.6 6.7 copy-start.26
  73.6 9.0 %copy-start.25 = (s32[2,2]{1,0:T(2,128)S(1)}, s32[2,2]{1,0:T(2,128)}, u32[]{:S(2)}) copy-start(s32[2,2]{1,0:T(2,128)} %get-tuple-element.20) | copy-start | bytes 52
  73.6 28.5 %copy-start.7 = (bf16[16,6,64,64]{3,2,1,0:T(8,128)(2,1)S(1)}, bf16[16,6,64,64]{3,2,1,0:T(8,128)(2,1)}, u32[]{:S(2)}) copy-start(bf16[16,6,64,64]{3,2,1,0:T(8,128)(2,1)} %custom-call.1) | copy-start | bytes 2359300
  75.9 4.4 collective-permute-start.5
  80.3 2.3 collective-permute-start.6
  82.6 5.1 collective-permute-start.9
  87.8 13.0 %collective-permute-start.1 = (s32[2,2]{1,0:T(2,128)}, s32[2,2]{1,0:T(2,128)S(1)}, u32[]{:S(2)}, u32[]{:S(2)}) collective-permute-start(s32[2,2]{1,0:T(2,128)} %collective-permute-done), channel_id=1, source_target_pairs={{1,0},{2,1},{3,2},{4,3},{5,4},{6,5},{7,6},{8,7},{9,8},{10,9},{11,1... | collective-permute-start | bytes 56 | tf_op jit(solution)/shard_map/ppermute | solution.py:15
  89.1 11.8 %collective-permute-start.4 = (s32[2,2]{1,0:T(2,128)}, s32[2,2]{1,0:T(2,128)S(1)}, u32[]{:S(2)}, u32[]{:S(2)}) collective-permute-start(s32[2,2]{1,0:T(2,128)} %collective-permute-done.3), channel_id=1, source_target_pairs={{0,1},{1,2},{2,3},{3,4},{4,5},{5,6},{6,7},{7,8},{8,9},{9,10},{10,1... | collective-permute-start | bytes 56 | tf_op jit(solution)/shard_map/ppermute | solution.py:15
  93.7 7.4 collective-permute-start.8
  95.0 6.6 collective-permute-start.11
  149.9 6.8 copy-start.5
  149.9 6.8 copy-start.12
  149.9 26.2 %copy-start.28 = (s32[1,1,8]{2,1,0:T(1,128)S(1)}, s32[1,1,8]{2,1,0:T(1,128)}, u32[]{:S(2)}) copy-start(s32[1,1,8]{2,1,0:T(1,128)} %param.11) | copy-start | bytes 100
  152.2 6.5 collective-permute-start.12
  158.7 48.1 %collective-permute-start.13 = (bf16[2,6,4096]{2,0,1:T(2,128)(2,1)}, bf16[2,6,4096]{2,0,1:T(2,128)(2,1)S(1)}, u32[]{:S(2)}, u32[]{:S(2)}) collective-permute-start(bf16[2,6,4096]{2,0,1:T(2,128)(2,1)} %collective-permute-done.12), channel_id=1, source_target_pairs={{0,16},{16,32},{32,48},{48,64},{64,80},{80,96},{96,112},{112,128},... | collective-permute-start | bytes 294920 | tf_op jit(solution)/shard_map/ppermute | solution.py:15
  188.9 3.9 copy-start.15
  188.9 6.1 copy-start.14
  188.9 7.7 copy-start.13
  193.1 21.1 %collective-permute-start.14 = (bf16[2,6,4096]{2,0,1:T(2,128)(2,1)S(1)}, bf16[2,6,4096]{2,0,1:T(2,128)(2,1)S(1)}, u32[]{:S(2)}, u32[]{:S(2)}) collective-permute-start(bf16[2,6,4096]{2,0,1:T(2,128)(2,1)S(1)} %copy.87), channel_id=1, source_target_pairs={{0,16},{16,32},{32,48},{48,64},{64,80},{80,96},{96,112},{112,128},... | collective-permute-start | bytes 294920 | tf_op jit(solution)/shard_map/ppermute | solution.py:15
  195.3 20.1 %collective-permute-start.15 = (bf16[2,6,4096]{2,0,1:T(2,128)(2,1)S(1)}, bf16[2,6,4096]{2,0,1:T(2,128)(2,1)S(1)}, u32[]{:S(2)}, u32[]{:S(2)}) collective-permute-start(bf16[2,6,4096]{2,0,1:T(2,128)(2,1)S(1)} %copy.88), channel_id=1, source_target_pairs={{1,0},{2,1},{3,2},{4,3},{5,4},{6,5},{7,6},{8,7},{9,8},{10,9},{11,1... | collective-permute-start | bytes 294920 | tf_op jit(solution)/shard_map/ppermute | solution.py:15
  197.0 32.0 %collective-permute-start.17 = (bf16[2,6,4096]{2,0,1:T(2,128)(2,1)S(1)}, bf16[2,6,4096]{2,0,1:T(2,128)(2,1)S(1)}, u32[]{:S(2)}, u32[]{:S(2)}) collective-permute-start(bf16[2,6,4096]{2,0,1:T(2,128)(2,1)S(1)} %copy.89), channel_id=1, source_target_pairs={{0,1},{1,2},{2,3},{3,4},{4,5},{5,6},{6,7},{7,8},{8,9},{9,10},{10,1... | collective-permute-start | bytes 294920 | tf_op jit(solution)/shard_map/ppermute | solution.py:15
  204.6 24.4 %collective-permute-start.18 = (bf16[2,6,4096]{2,0,1:T(2,128)(2,1)S(1)}, bf16[2,6,4096]{2,0,1:T(2,128)(2,1)S(1)}, u32[]{:S(2)}, u32[]{:S(2)}) collective-permute-start(bf16[2,6,4096]{2,0,1:T(2,128)(2,1)S(1)} %copy.90), channel_id=1, source_target_pairs={{1,0},{2,1},{3,2},{4,3},{5,4},{6,5},{7,6},{8,7},{9,8},{10,9},{11,1... | collective-permute-start | bytes 294920 | tf_op jit(solution)/shard_map/ppermute | solution.py:15
  206.8 12.8 %collective-permute-start.19 = (bf16[2,6,4096]{2,0,1:T(2,128)(2,1)S(1)}, bf16[2,6,4096]{2,0,1:T(2,128)(2,1)S(1)}, u32[]{:S(2)}, u32[]{:S(2)}) collective-permute-start(bf16[2,6,4096]{2,0,1:T(2,128)(2,1)S(1)} %copy.91), channel_id=1, source_target_pairs={{0,1},{1,2},{2,3},{3,4},{4,5},{5,6},{6,7},{7,8},{8,9},{9,10},{10,1... | collective-permute-start | bytes 294920 | tf_op jit(solution)/shard_map/ppermute | solution.py:15
  214.2 8.9 %collective-permute-start.22 = (bf16[2,6,4096]{2,0,1:T(2,128)(2,1)S(1)}, bf16[2,6,4096]{2,0,1:T(2,128)(2,1)S(1)}, u32[]{:S(2)}, u32[]{:S(2)}) collective-permute-start(bf16[2,6,4096]{2,0,1:T(2,128)(2,1)S(1)} %copy.93), channel_id=1, source_target_pairs={{1,0},{2,1},{3,2},{4,3},{5,4},{6,5},{7,6},{8,7},{9,8},{10,9},{11,1... | collective-permute-start | bytes 294920 | tf_op jit(solution)/shard_map/ppermute | solution.py:15
  215.5 11.5 %collective-permute-start.16 = (bf16[2,6,4096]{2,0,1:T(2,128)(2,1)S(1)}, bf16[2,6,4096]{2,0,1:T(2,128)(2,1)S(1)}, u32[]{:S(2)}, u32[]{:S(2)}) collective-permute-start(bf16[2,6,4096]{2,0,1:T(2,128)(2,1)S(1)} %collective-permute-done.15), channel_id=1, source_target_pairs={{0,16},{16,32},{32,48},{48,64},{64,80},{80,96},{96,112},{112,128},... | collective-permute-start | bytes 294920 | tf_op jit(solution)/shard_map/ppermute | solution.py:15
  219.6 10.7 %collective-permute-start.21 = (bf16[2,6,4096]{2,0,1:T(2,128)(2,1)S(1)}, bf16[2,6,4096]{2,0,1:T(2,128)(2,1)S(1)}, u32[]{:S(2)}, u32[]{:S(2)}) collective-permute-start(bf16[2,6,4096]{2,0,1:T(2,128)(2,1)S(1)} %copy.92), channel_id=1, source_target_pairs={{16,0},{32,16},{48,32},{64,48},{80,64},{96,80},{112,96},{128,112},... | collective-permute-start | bytes 294920 | tf_op jit(solution)/shard_map/ppermute | solution.py:15
  223.1 7.2 collective-permute-start.20
  227.0 5.9 collective-permute-start.23
  318.2 3.2 copy-start.2
  368.5 0.8 copy-start.22
  370.7 1.8 copy-start.6
  420.0 2.4 copy-start.21
  422.5 2.7 copy-start.3
  478.5 6.9 copy-start.16
  485.4 5.3 copy-start.4
  485.4 5.2 copy-start.18
  485.4 5.2 copy-start.30
  490.7 1.3 copy-start.10
  490.7 277.4 %copy-start.1 = (bf16[512,256]{1,0:T(8,128)(2,1)S(1)}, bf16[512,256]{1,0:T(8,128)(2,1)}, u32[]{:S(2)}) copy-start(bf16[512,256]{1,0:T(8,128)(2,1)} %param.16) | copy-start | bytes 786436
Sparse Core Ops, SparseCore 0:
  485.5 279.1 all-reduce.3
where the time goes:
time: 788 us; the launch traced here: 775 us
  local copies, waits for them, and re-layouts  352 us (45%)
  waiting for transfers between devices  178 us (23%)
  blocking collectives  105 us (13%)
  starting transfers between devices  89.9 us (11%)
  matrix products  32.7 us (4%)
  between operations  15.3 us (2%)
    psum x1, waiting for transfers between devices, per_device(): lax.psum((local_grads[0], local_grads[1], local_grads[2], local_grads[3])...  168 us
    psum x1, blocking collectives, per_device(): lax.psum((local_grads[0], local_grads[1], local_grads[2], local_grads[3])...  105 us
    ppermute x24, starting transfers between devices, shifted(): return lax.ppermute(block, axis, route)  89.8 us
    reshape x5, local copies, waits for them, and re-layouts, patchify(): blocks.reshape(channels * 4, batch_size * (rows_in // 2) * (cols_in // 2))  63.8 us
    transpose x4, local copies, waits for them, and re-layouts, unpatchify(): blocks = blocks.transpose(0, 3, 4, 1, 5, 2)  61.7 us
    transpose x4, local copies, waits for them, and re-layouts, patchify(): blocks = blocks.transpose(0, 3, 5, 1, 2, 4)  54.4 us
    gather x48, local copies, waits for them, and re-layouts  47.4 us
    reshape x4, local copies, waits for them, and re-layouts, unpatchify(): grads_in.reshape(channels, 2, 2, batch_size, rows_in // 2, cols_in // 2)  46 us
  transfers between devices with their start and end apart: 25, of which 9 were waited for; matrix products, arithmetic and copies ran while one was open for 10% of the time, Pallas kernels for 0%

commit v1 on v0

v1 whole, which is shorter than its diff:
```python
import functools

import jax
import jax.numpy as jnp
from jax import lax
from jax.experimental import pallas as pl
from jax.experimental.pallas import tpu as pltpu
from jax.sharding import PartitionSpec as P

DIRECTIONS = ((-1, -1), (-1, 0), (-1, 1), (0, -1), (0, 1), (1, -1), (1, 0), (1, 1))
MESH = pl.DeviceIdType.MESH
BF = jnp.bfloat16
F32 = jnp.float32
I32 = jnp.int32
VMEM_BYTES = 56 * 1024 * 1024
ROWS = 1536


def iota(shape, dim):
    return lax.broadcasted_iota(I32, shape, dim)


def one_hot(condition, kind=BF):
    return jnp.where(condition, 1.0, 0.0).astype(kind)


def nn(a, b):
    return lax.dot_general(a, b, (((1,), (0,)), ((), ())), preferred_element_type=F32)


def nt(a, b):
    return lax.dot_general(a, b, (((1,), (1,)), ((), ())), preferred_element_type=F32)


def tn(a, b):
    return lax.dot_general(a, b, (((0,), (0,)), ((), ())), preferred_element_type=F32)


def cut_kernel(off_ref, img_ref, got_ref, msg, req, rows_sel, rows_got, cut,
               req_send, req_recv, rep_send, rep_recv):
    ty = lax.axis_index("ty")
    tx = lax.axis_index("tx")
    n_ty = lax.axis_size("ty")
    n_tx = lax.axis_size("tx")

    def device(dy, dx):
        return (lax.rem(ty + dy + n_ty, n_ty), lax.rem(tx + dx + n_tx, n_tx))

    barrier = pltpu.get_barrier_semaphore()
    for dy, dx in DIRECTIONS:
        pl.semaphore_signal(barrier, inc=1, device_id=device(dy, dx), device_id_type=MESH)

    lane = iota((8, 128), 1)
    sub = iota((8, 128), 0)
    first = lane < 64
    col_step = 8 * (lane % 8) + (lane // 8) % 8
    for k in range(8):
        r0 = jnp.where(first, off_ref[k * 4], off_ref[k * 4 + 1])
        c0 = jnp.where(first, off_ref[k * 4 + 2], off_ref[k * 4 + 3] + 256)
        msg[k] = jnp.where(sub == 0, c0 + col_step, r0 + lane % 64)

    pl.semaphore_wait(barrier, 8)

    requests = []
    for k, (dy, dx) in enumerate(DIRECTIONS):
        copy = pltpu.make_async_remote_copy(
            src_ref=msg.at[k], dst_ref=req.at[k],
            send_sem=req_send.at[k], recv_sem=req_recv.at[k],
            device_id=device(dy, dx), device_id_type=MESH,
        )
        copy.start()
        requests.append(copy)
    for copy in requests:
        copy.wait()

    for k in range(8):
        rows_sel[:, k * 128:(k + 1) * 128] = one_hot(iota((128, 128), 0) == req[k][1:2, :])
    for band in range(6):
        rows_got[band] = tn(rows_sel[...], img_ref[band])

    replies = []
    for k in (0, 2, 5, 7, 3, 4, 1, 6):
        dy, dx = DIRECTIONS[k]
        halves = []
        for p in range(2):
            pieces = []
            for block in range(8):
                at = k * 128 + p * 64 + block * 8
                for band in range(6):
                    pieces.append(rows_got[band, at:at + 8, :])
            halves.append(jnp.concatenate(pieces, axis=0).astype(BF))
        cols_sel = one_hot(iota((512, 128), 0) == req[k][0:1, :])
        cut[k] = (nn(halves[0], cols_sel[:256]) + nn(halves[1], cols_sel[256:])).astype(BF)
        copy = pltpu.make_async_remote_copy(
            src_ref=cut.at[k], dst_ref=got_ref.at[k],
            send_sem=rep_send.at[k], recv_sem=rep_recv.at[k],
            device_id=device(-dy, -dx), device_id_type=MESH,
        )
        copy.start()
        replies.append(copy)
    for copy in replies:
        copy.wait()


def exchange_cutouts(offsets, image):
    return pl.pallas_call(
        cut_kernel,
        out_shape=jax.ShapeDtypeStruct((8, 384, 128), BF),
        in_specs=[pl.BlockSpec(memory_space=pltpu.SMEM), pl.BlockSpec(memory_space=pltpu.VMEM)],
        out_specs=pl.BlockSpec(memory_space=pltpu.VMEM),
        scratch_shapes=[
            pltpu.VMEM((8, 8, 128), I32),
            pltpu.VMEM((8, 8, 128), I32),
            pltpu.VMEM((128, 1024), BF),
            pltpu.VMEM((6, 1024, 256), F32),
            pltpu.VMEM((8, 384, 128), BF),
            pltpu.SemaphoreType.DMA((8,)),
            pltpu.SemaphoreType.DMA((8,)),
            pltpu.SemaphoreType.DMA((8,)),
            pltpu.SemaphoreType.DMA((8,)),
        ],
        compiler_params=pltpu.CompilerParams(
            collective_id=0, has_side_effects=True, vmem_limit_bytes=VMEM_BYTES
        ),
        name="cutouts",
    )(offsets, image)


def first_mask():
    row = iota((512, 192), 0)
    col = iota((512, 192), 1)
    return (row // 128 == (col % 8) // 2) & ((row // 64) % 2 == col // 96)


def first_spread():
    row = iota((24, 192), 0)
    col = iota((24, 192), 1)
    return row == ((col % 48) // 8) * 4 + (col % 2) * 2 + (col // 48) % 2


def net_kernel(cnt_ref, img_ref, got_ref, own_target_ref, cut_target_ref, w1_ref, w2_ref, w3_ref, wh_ref,
               grads_ref, cut_pred_ref,
               field, place, wide1, w2, w2t, w3, w3t, act1, slope1, act2, slope2, delta1, delta2,
               target, mask, pred_all, g1, g2, g3, gh):
    up = one_hot(iota((512, 64), 0) % 64 == iota((512, 64), 1))
    wide = nn(nt(up, w1_ref[...]).astype(BF), one_hot(first_spread()))
    wide1[...] = jnp.where(first_mask(), wide, 0.0).astype(BF)
    new = iota((256, 256), 0)
    w2[...] = nn(one_hot(iota((256, 256), 1) == (new % 64) * 4 + new // 64), w2_ref[...]).astype(BF)
    new = iota((256, 256), 1)
    w2t[...] = tn(w2_ref[...], one_hot(iota((256, 256), 0) == (new % 64) * 4 + new // 64)).astype(BF)
    new = iota((512, 512), 0)
    w3[...] = nn(one_hot(iota((512, 512), 1) == (new % 128) * 4 + new // 128), w3_ref[...]).astype(BF)
    new = iota((512, 512), 1)
    w3t[...] = tn(w3_ref[...], one_hot(iota((512, 512), 0) == (new % 128) * 4 + new // 128)).astype(BF)
    wh = wh_ref[...]

    src = iota((1024, 1024), 0)
    place[...] = one_hot(iota((1024, 1024), 1) == (src % 8) * 128 + (src // 256) * 32 + (src % 256) // 8)
    lines = []
    images = [img_ref[band].astype(F32) for band in range(6)]
    for q in range(4):
        for band in range(6):
            lines.append(jnp.concatenate(
                [images[band][(4 * q + r) * 8:(4 * q + r) * 8 + 8] for r in range(4)], axis=1))
    spread = nn(jnp.concatenate(lines, axis=0).astype(BF), place[...]).astype(BF)
    for q in range(4):
        for j in range(8):
            field[j // 4, 0, (j % 4) * 48:(j % 4) * 48 + 48, q * 128:(q + 1) * 128] = (
                spread[q * 48:(q + 1) * 48, j * 128:(j + 1) * 128])
    src = iota((1024, 1024), 0)
    place[...] = one_hot(
        iota((1024, 1024), 1)
        == ((src // 8) % 8) * 128 + ((src // 64) % 2) * 64 + (src // 128) * 8 + src % 8)
    for half in range(2):
        stack = jnp.concatenate(
            [jnp.concatenate([got_ref[half * 4 + k, r * 48:(r + 1) * 48, :] for r in range(8)], axis=1)
             for k in range(4)], axis=0)
        spread = nn(stack, place[...]).astype(BF)
        for k in range(4):
            for j in range(8):
                field[j // 4, 1 + half, (j % 4) * 48:(j % 4) * 48 + 48, k * 128:(k + 1) * 128] = (
                    spread[k * 48:(k + 1) * 48, j * 128:(j + 1) * 128])

    target[0] = own_target_ref[...]
    target[1] = cut_target_ref[:, :512]
    target[2] = cut_target_ref[:, 512:]
    mask[0] = jnp.full((8, 512), 1.0, F32)
    slot = (iota((8, 128), 1) // 64)
    for k in range(8):
        mask[1 + k // 4, :, (k % 4) * 128:(k % 4) * 128 + 128] = jnp.where(slot < cnt_ref[k], 1.0, 0.0)

    g1[...] = jnp.zeros_like(g1)
    g2[...] = jnp.zeros_like(g2)
    g3[...] = jnp.zeros_like(g3)
    gh[...] = jnp.zeros_like(gh)

    def silu(pre):
        sig = 0.5 * jnp.tanh(0.5 * pre) + 0.5
        act = pre * sig
        return act.astype(BF), sig + act * (1.0 - sig)

    def part(step, carry):
        for ac in range(2):
            act1[ac], slope1[ac] = silu(nn(wide1[...], field[ac, step]))
            for ar in range(2):
                at = (ar * 2 + ac) * 128
                act2[at:at + 128], slope2[at:at + 128] = silu(nn(w2t[...], act1[ac, ar * 256:ar * 256 + 256]))
        act3, slope3 = silu(nn(w3t[...], act2[...]))
        pred = nn(wh, act3)
        used = mask[step]
        grad = ((pred - target[step]) * used * (1.0 / 256.0)).astype(BF)
        pred_all[step] = (pred * used)
        gh[...] += nt(grad, act3)
        delta3 = (tn(wh, grad) * slope3).astype(BF)
        g3[...] += nt(act2[...], delta3)
        delta2[...] = (nn(w3[...], delta3) * slope2[...]).astype(BF)
        for ac in range(2):
            for ar in range(2):
                at = (ar * 2 + ac) * 128
                rows = slice(ar * 256, ar * 256 + 256)
                g2[...] += nt(act1[ac, rows], delta2[at:at + 128])
                delta1[ac, rows] = (nn(w2[...], delta2[at:at + 128]) * slope1[ac, rows]).astype(BF)
            g1[...] += nt(delta1[ac], field[ac, step])
        return carry

    lax.fori_loop(0, 3, part, 0)

    cut_pred_ref[:, :512] = pred_all[1].astype(BF)
    cut_pred_ref[:, 512:] = pred_all[2].astype(BF)

    for phase in range(4):
        for half in range(2):
            grads_ref[pl.ds(half * 512 + phase, 128, stride=4), :] = (
                g3[phase * 128:phase * 128 + 128, half * 128:half * 128 + 128])
        grads_ref[pl.ds(1024 + phase, 64, stride=4), :] = g2[phase * 64:phase * 64 + 64, :]
    picked = jnp.where(first_mask(), g1[...], 0.0)
    folded = lax.dot_general(
        one_hot(first_spread(), F32), picked, (((1,), (1,)), ((), ())),
        precision=lax.Precision.HIGHEST, preferred_element_type=F32)
    total = lax.dot_general(
        folded, one_hot(iota((512, 128), 0) % 64 == iota((512, 128), 1), F32), (((1,), (0,)), ((), ())),
        precision=lax.Precision.HIGHEST, preferred_element_type=F32)
    grads_ref[1280:1304, :] = total
    grads_ref[1304:1312, :] = gh[:, :128]
    grads_ref[1312:1320, :] = gh[:, 128:]
    grads_ref[1320:, :] = jnp.zeros((ROWS - 1320, 128), F32)


def network(counts, image, got, own_target, cut_target, weights):
    vmem = pl.BlockSpec(memory_space=pltpu.VMEM)
    return pl.pallas_call(
        net_kernel,
        out_shape=(jax.ShapeDtypeStruct((ROWS, 128), F32), jax.ShapeDtypeStruct((8, 1024), BF)),
        in_specs=[pl.BlockSpec(memory_space=pltpu.SMEM)] + [vmem] * 8,
        out_specs=(vmem, vmem),
        scratch_shapes=[
            pltpu.VMEM((2, 3, 192, 512), BF),
            pltpu.VMEM((1024, 1024), BF),
            pltpu.VMEM((512, 192), BF),
            pltpu.VMEM((256, 128), BF),
            pltpu.VMEM((128, 256), BF),
            pltpu.VMEM((512, 256), BF),
            pltpu.VMEM((256, 512), BF),
            pltpu.VMEM((2, 512, 512), BF),
            pltpu.VMEM((2, 512, 512), F32),
            pltpu.VMEM((512, 512), BF),
            pltpu.VMEM((512, 512), F32),
            pltpu.VMEM((2, 512, 512), BF),
            pltpu.VMEM((512, 512), BF),
            pltpu.VMEM((3, 8, 512), F32),
            pltpu.VMEM((3, 8, 512), F32),
            pltpu.VMEM((3, 8, 512), F32),
            pltpu.VMEM((512, 192), F32),
            pltpu.VMEM((256, 128), F32),
            pltpu.VMEM((512, 256), F32),
            pltpu.VMEM((8, 256), F32),
        ],
        compiler_params=pltpu.CompilerParams(vmem_limit_bytes=VMEM_BYTES),
        name="network",
    )(counts, image, got, own_target, cut_target, *weights)


def sum_kernel(p_ref, o1_ref, o2_ref, o3_ref, oh_ref,
               from_core, held_core, from_x, held_x, from_z, held_z, from_y, full, send, recv):
    ty = lax.axis_index("ty")
    tx = lax.axis_index("tx")
    core = ty % 2
    x = (ty // 2) % 4
    z = (tx // 4) * 2 + ty // 8
    y = tx % 4

    def device(core_at, x_at, y_at, z_at):
        return ((z_at % 2) * 8 + x_at * 2 + core_at, (z_at // 2) * 4 + y_at)

    def core_peer(d):
        return device(1 - core, x, y, z)

    def x_peer(d):
        return device(core, (x + d) % 4, y, z)

    def y_peer(d):
        return device(core, x, (y + d) % 4, z)

    def z_peer(d):
        return device(core, x, y, (z + d) % 8)

    barrier = pltpu.get_barrier_semaphore()
    for peer, count in ((core_peer, 2), (x_peer, 4), (y_peer, 4), (z_peer, 8)):
        for d in range(1, count):
            pl.semaphore_signal(barrier, inc=1, device_id=peer(d), device_id_type=MESH)
    pl.semaphore_wait(barrier, 14)

    counter = [0]

    def push(src, dst, peer):
        copy = pltpu.make_async_remote_copy(
            src_ref=src, dst_ref=dst, send_sem=send.at[counter[0]], recv_sem=recv.at[counter[0]],
            device_id=peer, device_id_type=MESH)
        counter[0] += 1
        copy.start()
        return copy

    def finish(copies):
        for copy in copies:
            copy.wait()

    def rows(at, count):
        return pl.ds(pl.multiple_of(at, 8), count)

    finish([push(p_ref.at[rows((1 - core) * 768, 768)], from_core, core_peer(1))])
    held_core[...] = p_ref[rows(core * 768, 768), :] + from_core[...]
    finish([push(held_core.at[rows((x + d) % 4 * 192, 192)], from_x.at[d - 1], x_peer(d)) for d in range(1, 4)])
    held_x[...] = held_core[rows(x * 192, 192), :] + from_x[0] + from_x[1] + from_x[2]
    finish([push(held_x.at[rows((z + d) % 8 * 24, 24)], from_z.at[d - 1], z_peer(d)) for d in range(1, 8)])
    total = held_x[rows(z * 24, 24), :]
    for d in range(7):
        total = total + from_z[d]
    held_z[...] = total
    from_y[y] = total
    finish([push(held_z, from_y.at[y], y_peer(d)) for d in range(1, 4)])
    at_z = core * 768 + x * 192 + z * 24
    full[rows(at_z, 24), :] = from_y[0] + from_y[1] + from_y[2] + from_y[3]
    finish([push(full.at[rows(at_z, 24)], full.at[rows(at_z, 24)], z_peer(d)) for d in range(1, 8)])
    at_x = core * 768 + x * 192
    finish([push(full.at[rows(at_x, 192)], full.at[rows(at_x, 192)], x_peer(d)) for d in range(1, 4)])
    at_core = core * 768
    finish([push(full.at[rows(at_core, 768)], full.at[rows(at_core, 768)], core_peer(1))])

    o3_ref[:, :128] = full[0:512, :]
    o3_ref[:, 128:] = full[512:1024, :]
    o2_ref[...] = full[1024:1280, :]
    o1_ref[...] = full[1280:1304, :64]
    oh_ref[:, :128] = full[1304:1312, :]
    oh_ref[:, 128:] = full[1312:1320, :]


def sum_everywhere(packed):
    vmem = pl.BlockSpec(memory_space=pltpu.VMEM)
    return pl.pallas_call(
        sum_kernel,
        out_shape=(
            jax.ShapeDtypeStruct((24, 64), F32),
            jax.ShapeDtypeStruct((256, 128), F32),
            jax.ShapeDtypeStruct((512, 256), F32),
            jax.ShapeDtypeStruct((8, 256), F32),
        ),
        in_specs=[vmem],
        out_specs=(vmem,) * 4,
        scratch_shapes=[
            pltpu.VMEM((768, 128), F32),
            pltpu.VMEM((768, 128), F32),
            pltpu.VMEM((3, 192, 128), F32),
            pltpu.VMEM((192, 128), F32),
            pltpu.VMEM((7, 24, 128), F32),
            pltpu.VMEM((24, 128), F32),
            pltpu.VMEM((4, 24, 128), F32),
            pltpu.VMEM((ROWS, 128), F32),
            pltpu.SemaphoreType.DMA((25,)),
            pltpu.SemaphoreType.DMA((25,)),
        ],
        compiler_params=pltpu.CompilerParams(
            collective_id=1, has_side_effects=True, vmem_limit_bytes=VMEM_BYTES
        ),
        name="sums",
    )(packed)


def per_device(sky_tile, request_offset, request_count, tile_target, cut_target, w_first, w_second, w_third, w_head):
    got = exchange_cutouts(request_offset.reshape(-1), sky_tile)
    packed, cut_pred = network(
        request_count.reshape(-1), sky_tile, got, tile_target[0, 0], cut_target[0, 0],
        (w_first, w_second, w_third, w_head))
    return (*sum_everywhere(packed), cut_pred[None, None])


def solution(mesh):
    return jax.shard_map(
        per_device,
        mesh=mesh,
        in_specs=(
            P(None, "ty", "tx"),
            P("ty", "tx", None, None, None),
            P("ty", "tx", None),
            P("ty", "tx", None, None),
            P("ty", "tx", None, None),
            P(),
            P(),
            P(),
            P(),
        ),
        out_specs=(P(), P(), P(), P(), P("ty", "tx", None, None)),
        check_vma=False,
    )
```

time: 788 us -> 93.8 us (0.12); the launches traced: 775 us -> 93.5 us
  local copies, waits for them, and re-layouts: 352 us -> 6.73 us
  waiting for transfers between devices: 178 us -> 0 us
  blocking collectives: 105 us -> 0 us
  starting transfers between devices: 89.9 us -> 0 us
  Pallas kernels: 0 us -> 86.2 us
  matrix products: 32.7 us -> 0 us
  between operations: 15.3 us -> 0.66 us
    psum x1 -> x0, waiting for transfers between devices: 168 us -> none  [per_device(): lax.psum((local_grads[0], local_grads[1], local_grads[2], local_grads[3])...]
    reshape x12 -> x1, local copies, waits for them, and re-layouts: 122 us -> 0.61 us  [per_device(): got = exchange_cutouts(request_offset.reshape(-1), sky_tile)]
    transpose x9 -> x0, local copies, waits for them, and re-layouts: 121 us -> none  [the longest x4 61.7 us: unpatchify(): blocks = blocks.transpose(0, 3, 4, 1, 5, 2)]
    psum x1 -> x0, blocking collectives: 105 us -> none  [per_device(): lax.psum((local_grads[0], local_grads[1], local_grads[2], local_grads[3])...]
    ppermute x24 -> x0, starting transfers between devices: 89.8 us -> none  [shifted(): return lax.ppermute(block, axis, route)]
    pallas_call x0 -> x3, Pallas kernels: none -> 86.2 us  [the longest x1 37.3 us: sum_everywhere(): pl.pallas_call(sum_kernel, out_shape=(jax.ShapeDtypeStruct((24, 64), F32)...]
    gather x48 -> x0, local copies, waits for them, and re-layouts: 47.4 us -> none
    dot_general x22 -> x0, matrix products: 32.7 us -> none  [the longest x8 14.4 us: inner(): lax.dot_general(left_mat, right_mat, (((0,), (0,)), ((), ())), preferred_...]
  transfers between devices with their start and end apart: 25 -> 0, of which waited for: 9 -> 0; matrix products, arithmetic and copies ran while one was open for 10% -> 0% of each run, Pallas kernels for 0% -> 0%
where the time goes in v1:
time: 93.8 us; the launch traced here: 93.5 us
  Pallas kernels  86.2 us (92%)
  local copies, waits for them, and re-layouts  6.73 us (7%)
    pallas_call x1, Pallas kernels, sum_everywhere(): pl.pallas_call(sum_kernel, out_shape=(jax.ShapeDtypeStruct((24, 64), F32)...  37.3 us
    pallas_call x1, Pallas kernels, exchange_cutouts(): pl.pallas_call(cut_kernel, out_shape=jax.ShapeDtypeStruct((8, 384, 128),...  34.6 us
    pallas_call x1, Pallas kernels, network(): pl.pallas_call(net_kernel, out_shape=(jax.ShapeDtypeStruct((ROWS, 128), F...  14.3 us
    unnamed x9, local copies, waits for them, and re-layouts  6.12 us

profile of v1, /device:TPU:1, one launch (start us, length us, event | category | flops | bytes accessed | tf_op | source)
XLA Modules:
  0.0 93.5 jit_solution(8279887475863521769)
XLA Ops:
  0.6 0.0 copy-start.1
  0.6 0.7 copy-done.1
  1.3 0.1 copy.15
  1.4 0.6 reshape.17.off_ref
  2.0 34.6 %cutouts.1.got_ref = bf16[8,384,128]{2,1,0:T(8,128)(2,1)} custom-call(s32[32]{0:T(128)} %reshape.17.off_ref, bf16[6,128,256]{2,1,0:T(8,128)(2,1)} %img_ref.3), custom_call_target="tpu_custom_call" | custom-call | tf_op jit(solution)/shard_map/cutouts/pallas_call | solution.py:106
  36.6 14.3 %network.1 = (f32[1536,128]{1,0:T(8,128)}, bf16[8,1024]{1,0:T(8,128)(2,1)}) custom-call(s32[8]{0:T(128)} %bitcast.6, bf16[6,128,256]{2,1,0:T(8,128)(2,1)} %img_ref.3, bf16[8,384,128]{2,1,0:T(8,128)(2,1)} %cutouts.1.got_ref, f32[8,512]{1,0:T(8,128)} %bitcast.5, f32[8,1024]{1,0:T(8,128)} %bitcast.4, bf16[24,64]{1,0:T(8,128)(2,1)} %w1_ref.1, ...), custom_call_target="tpu_custom_call" | custom-call | tf_op jit(solution)/shard_map/network/pallas_call | solution.py:252
  50.9 37.3 %sums.1 = (f32[24,64]{1,0:T(8,128)}, f32[256,128]{1,0:T(8,128)}, f32[512,256]{1,0:T(8,128)}, f32[8,256]{1,0:T(8,128)}) custom-call(f32[1536,128]{1,0:T(8,128)} %get-tuple-element.11.p_ref), custom_call_target="tpu_custom_call" | custom-call | tf_op jit(solution)/shard_map/sums/pallas_call | solution.py:360
  88.2 1.3 %copy.20 = f32[24,64]{1,0:T(8,128)} copy(f32[24,64]{1,0:T(8,128)} %get-tuple-element.22) | data formatting | bytes 12288
  89.5 1.6 %copy.21 = f32[256,128]{1,0:T(8,128)} copy(f32[256,128]{1,0:T(8,128)} %get-tuple-element.23) | data formatting | bytes 262144
  91.1 0.0 copy-start
  91.1 1.9 %copy.22 = f32[512,256]{1,0:T(8,128)} copy(f32[512,256]{1,0:T(8,128)} %get-tuple-element.24) | data formatting | bytes 1048576
  92.9 0.0 copy-done
  93.0 0.6 copy.23
Async XLA Ops:
  0.6 0.7 copy-start.1
  91.1 1.9 %copy-start = (f32[8,256]{1,0:T(8,128)S(1)}, f32[8,256]{1,0:T(8,128)}, u32[]{:S(2)}) copy-start(f32[8,256]{1,0:T(8,128)} %get-tuple-element.25) | copy-start | bytes 24580

commit v2 on v1

v2 whole, which is shorter than its diff:
```python
import functools

import jax
import jax.numpy as jnp
from jax import lax
from jax.experimental import pallas as pl
from jax.experimental.pallas import tpu as pltpu
from jax.sharding import PartitionSpec as P

DIRECTIONS = ((-1, -1), (-1, 0), (-1, 1), (0, -1), (0, 1), (1, -1), (1, 0), (1, 1))
MESH = pl.DeviceIdType.MESH
BF = jnp.bfloat16
F32 = jnp.float32
I32 = jnp.int32
VMEM_BYTES = 56 * 1024 * 1024
ROWS = 1536


def iota(shape, dim):
    return lax.broadcasted_iota(I32, shape, dim)


def one_hot(condition, kind=BF):
    return jnp.where(condition, 1.0, 0.0).astype(kind)


def nn(a, b):
    return lax.dot_general(a, b, (((1,), (0,)), ((), ())), preferred_element_type=F32)


def nt(a, b):
    return lax.dot_general(a, b, (((1,), (1,)), ((), ())), preferred_element_type=F32)


def tn(a, b):
    return lax.dot_general(a, b, (((0,), (0,)), ((), ())), preferred_element_type=F32)


def first_mask():
    row = iota((512, 192), 0)
    col = iota((512, 192), 1)
    return ((row >> 7) == ((col & 7) >> 1)) & (((row >> 6) & 1) == jnp.where(col < 96, 0, 1))


def first_spread():
    row = iota((24, 192), 0)
    col = iota((24, 192), 1)
    return row == ((col % 48) // 8) * 4 + (col & 1) * 2 + ((col // 48) & 1)


def silu(pre):
    sig = 0.5 * jnp.tanh(0.5 * pre) + 0.5
    act = pre * sig
    return act.astype(BF), sig + act * (1.0 - sig)


def pick(flag, yes, no):
    return jnp.where(flag, jnp.int32(yes), jnp.int32(no))


def step_of(k):
    at = k + jnp.where(k >= 4, 1, 0)
    return at // 3 - 1, at % 3 - 1


def net_kernel(cnt_ref, off_ref, img_ref, own_target_ref, cut_target_ref, w1_ref, w2_ref, w3_ref, wh_ref,
               grads_ref, cut_pred_ref,
               msg, req, rows_sel, rows_got, cut, got,
               field, place_own, place_cut, wide1, w2, w2t, w3, w3t,
               act1, slope1, act2, slope2, delta1, delta2,
               target, mask, g1, g2, g3, gh,
               req_send, req_recv, rep_send, rep_recv):
    ty = lax.axis_index("ty")
    tx = lax.axis_index("tx")
    n_ty = lax.axis_size("ty")
    n_tx = lax.axis_size("tx")
    upper = (tx % 4) >= 2

    def device(dy, dx):
        return (lax.rem(ty + dy + n_ty, n_ty), lax.rem(tx + dx + n_tx, n_tx))

    barrier = pltpu.get_barrier_semaphore()
    for dy, dx in DIRECTIONS:
        pl.semaphore_signal(barrier, inc=1, device_id=device(dy, dx), device_id_type=MESH)

    lane = iota((8, 128), 1)
    sub = iota((8, 128), 0)
    first = lane < 64
    col_step = 8 * (lane & 7) + ((lane >> 3) & 7)
    row_step = lane & 63

    def offset(coord, p, k):
        return jnp.broadcast_to(off_ref[0, 0, coord, p:p + 1, k:k + 1], (8, 128))

    for k in range(8):
        r0 = jnp.where(first, offset(0, 0, k), offset(0, 1, k))
        c0 = jnp.where(first, offset(1, 0, k), offset(1, 1, k) + 256)
        msg[k] = jnp.where(sub == 0, c0 + col_step, r0 + row_step)

    pl.semaphore_wait(barrier, 8)

    requests = []
    for k, (dy, dx) in enumerate(DIRECTIONS):
        copy = pltpu.make_async_remote_copy(
            src_ref=msg.at[k], dst_ref=req.at[k],
            send_sem=req_send.at[k], recv_sem=req_recv.at[k],
            device_id=device(dy, dx), device_id_type=MESH,
        )
        copy.start()
        requests.append(copy)

    lanes = iota((1024, 128), 1)
    src = iota((1024, 128), 0)
    goal = (src & 7) * 128 + (src >> 8) * 32 + ((src & 255) >> 3)
    for j in range(8):
        place_own[:, j * 128:(j + 1) * 128] = one_hot(lanes + j * 128 == goal)
    src = iota((1024, 128), 0)
    goal = ((src >> 3) & 7) * 128 + ((src >> 6) & 1) * 64 + (src >> 7) * 8 + (src & 7)
    for j in range(8):
        place_cut[:, j * 128:(j + 1) * 128] = one_hot(lanes + j * 128 == goal)

    for copy in requests:
        copy.wait()

    for k in range(8):
        rows_sel[:, k * 128:(k + 1) * 128] = one_hot(iota((128, 128), 0) == req[k][1:2, :])
    for band in range(6):
        rows_got[band] = tn(rows_sel[...], img_ref[band])

    def reply(k):
        dy, dx = step_of(k)
        return pltpu.make_async_remote_copy(
            src_ref=cut.at[k], dst_ref=got.at[k],
            send_sem=rep_send.at[k], recv_sem=rep_recv.at[k],
            device_id=device(-dy, -dx), device_id_type=MESH,
        )

    for k_upper, k_lower in ((0, 2), (3, 4), (5, 7), (2, 0), (4, 3), (7, 5), (1, 1), (6, 6)):
        k = pick(upper, k_upper, k_lower)
        halves = []
        for p in range(2):
            pieces = []
            for block in range(8):
                at = pl.multiple_of(k * 128 + (p * 64 + block * 8), 8)
                for band in range(6):
                    pieces.append(rows_got[band, pl.ds(at, 8), :])
            halves.append(jnp.concatenate(pieces, axis=0).astype(BF))
        cols_sel = one_hot(iota((512, 128), 0) == req[k][0:1, :])
        cut[k] = (nn(halves[0], cols_sel[:256]) + nn(halves[1], cols_sel[256:])).astype(BF)
        reply(k).start()

    up = one_hot((iota((512, 64), 0) & 63) == iota((512, 64), 1))
    wide = nn(nt(up, w1_ref[...]).astype(BF), one_hot(first_spread()))
    wide1[...] = jnp.where(first_mask(), wide, 0.0).astype(BF)
    new = iota((256, 256), 0)
    w2[...] = nn(one_hot(iota((256, 256), 1) == (new & 63) * 4 + (new >> 6)), w2_ref[...]).astype(BF)
    new = iota((256, 256), 1)
    w2t[...] = tn(w2_ref[...], one_hot(iota((256, 256), 0) == (new & 63) * 4 + (new >> 6))).astype(BF)
    new = iota((512, 512), 0)
    w3[...] = nn(one_hot(iota((512, 512), 1) == (new & 127) * 4 + (new >> 7)), w3_ref[...]).astype(BF)
    new = iota((512, 512), 1)
    w3t[...] = tn(w3_ref[...], one_hot(iota((512, 512), 0) == (new & 127) * 4 + (new >> 7))).astype(BF)
    wh = wh_ref[...]

    lines = []
    images = [img_ref[band].astype(F32) for band in range(6)]
    for q in range(4):
        for band in range(6):
            lines.append(jnp.concatenate(
                [images[band][(4 * q + r) * 8:(4 * q + r) * 8 + 8] for r in range(4)], axis=1))
    spread = nn(jnp.concatenate(lines, axis=0).astype(BF), place_own[...]).astype(BF)
    for q in range(4):
        for j in range(8):
            field[j // 4, (j % 4) * 48:(j % 4) * 48 + 48, q * 128:(q + 1) * 128] = (
                spread[q * 48:(q + 1) * 48, j * 128:(j + 1) * 128])

    target[...] = own_target_ref[...]
    mask[...] = jnp.full((8, 512), 1.0, F32)
    g1[...] = jnp.zeros_like(g1)
    g2[...] = jnp.zeros_like(g2)
    g3[...] = jnp.zeros_like(g3)
    gh[...] = jnp.zeros_like(gh)

    def slot_of(step, at):
        early = pick(upper, (0, 3, 5, 1)[at], (2, 4, 7, 1)[at])
        late = pick(upper, (6, 2, 4, 7)[at], (6, 0, 3, 5)[at])
        return jnp.where(step == 1, early, late)

    def part(step, carry):
        @pl.when(step > 0)
        def cutouts():
            stack = []
            for at in range(4):
                k = slot_of(step, at)
                reply(k).wait_recv()
                stack.append(jnp.concatenate([got[k, r * 48:(r + 1) * 48, :] for r in range(8)], axis=1))
                here = slice(at * 128, at * 128 + 128)
                target[:, here] = cut_target_ref[:, pl.ds(pl.multiple_of(k * 128, 128), 128)]
                mask[:, here] = jnp.where((iota((8, 128), 1) >> 6) < cnt_ref[k], 1.0, 0.0)
            spread = nn(jnp.concatenate(stack, axis=0), place_cut[...]).astype(BF)
            for at in range(4):
                for j in range(8):
                    field[j // 4, (j % 4) * 48:(j % 4) * 48 + 48, at * 128:(at + 1) * 128] = (
                        spread[at * 48:(at + 1) * 48, j * 128:(j + 1) * 128])

        for ac in range(2):
            act1[ac], slope1[ac] = silu(nn(wide1[...], field[ac]))
            for ar in range(2):
                at = (ar * 2 + ac) * 128
                act2[at:at + 128], slope2[at:at + 128] = silu(nn(w2t[...], act1[ac, ar * 256:ar * 256 + 256]))
        act3, slope3 = silu(nn(w3t[...], act2[...]))
        pred = nn(wh, act3)
        grad = ((pred - target[...]) * mask[...] * (1.0 / 256.0)).astype(BF)

        @pl.when(step > 0)
        def predictions():
            shown = (pred * mask[...]).astype(BF)
            for at in range(4):
                k = slot_of(step, at)
                cut_pred_ref[:, pl.ds(pl.multiple_of(k * 128, 128), 128)] = shown[:, at * 128:at * 128 + 128]

        gh[...] += nt(grad, act3)
        delta3 = (tn(wh, grad) * slope3).astype(BF)
        g3[...] += nt(act2[...], delta3)
        delta2[...] = (nn(w3[...], delta3) * slope2[...]).astype(BF)
        for ac in range(2):
            for ar in range(2):
                at = (ar * 2 + ac) * 128
                rows = slice(ar * 256, ar * 256 + 256)
                g2[...] += nt(act1[ac, rows], delta2[at:at + 128])
                delta1[ac, rows] = (nn(w2[...], delta2[at:at + 128]) * slope1[ac, rows]).astype(BF)
            g1[...] += nt(delta1[ac], field[ac])
        return carry

    lax.fori_loop(0, 3, part, 0)

    for phase in range(4):
        for half in range(2):
            grads_ref[pl.ds(half * 512 + phase, 128, stride=4), :] = (
                g3[phase * 128:phase * 128 + 128, half * 128:half * 128 + 128])
        grads_ref[pl.ds(1024 + phase, 64, stride=4), :] = g2[phase * 64:phase * 64 + 64, :]
    picked = jnp.where(first_mask(), g1[...], 0.0)
    folded = lax.dot_general(
        one_hot(first_spread(), F32), picked, (((1,), (1,)), ((), ())),
        precision=lax.Precision.HIGHEST, preferred_element_type=F32)
    total = lax.dot_general(
        folded, one_hot((iota((512, 128), 0) & 63) == iota((512, 128), 1), F32), (((1,), (0,)), ((), ())),
        precision=lax.Precision.HIGHEST, preferred_element_type=F32)
    grads_ref[1280:1304, :] = total
    grads_ref[1304:1312, :] = gh[:, :128]
    grads_ref[1312:1320, :] = gh[:, 128:]
    grads_ref[1320:, :] = jnp.zeros((ROWS - 1320, 128), F32)

    for k in range(8):
        reply(jnp.int32(k)).wait_send()


def network(counts, offsets, image, own_target, cut_target, weights):
    vmem = pl.BlockSpec(memory_space=pltpu.VMEM)
    dma = pltpu.SemaphoreType.DMA((8,))
    return pl.pallas_call(
        net_kernel,
        out_shape=(jax.ShapeDtypeStruct((ROWS, 128), F32), jax.ShapeDtypeStruct((8, 1024), BF)),
        in_specs=[pl.BlockSpec(memory_space=pltpu.SMEM)] + [vmem] * 8,
        out_specs=(vmem, vmem),
        scratch_shapes=[
            pltpu.VMEM((8, 8, 128), I32),
            pltpu.VMEM((8, 8, 128), I32),
            pltpu.VMEM((128, 1024), BF),
            pltpu.VMEM((6, 1024, 256), F32),
            pltpu.VMEM((8, 384, 128), BF),
            pltpu.VMEM((8, 384, 128), BF),
            pltpu.VMEM((2, 192, 512), BF),
            pltpu.VMEM((1024, 1024), BF),
            pltpu.VMEM((1024, 1024), BF),
            pltpu.VMEM((512, 192), BF),
            pltpu.VMEM((256, 128), BF),
            pltpu.VMEM((128, 256), BF),
            pltpu.VMEM((512, 256), BF),
            pltpu.VMEM((256, 512), BF),
            pltpu.VMEM((2, 512, 512), BF),
            pltpu.VMEM((2, 512, 512), F32),
            pltpu.VMEM((512, 512), BF),
            pltpu.VMEM((512, 512), F32),
            pltpu.VMEM((2, 512, 512), BF),
            pltpu.VMEM((512, 512), BF),
            pltpu.VMEM((8, 512), F32),
            pltpu.VMEM((8, 512), F32),
            pltpu.VMEM((512, 192), F32),
            pltpu.VMEM((256, 128), F32),
            pltpu.VMEM((512, 256), F32),
            pltpu.VMEM((8, 256), F32),
            dma, dma, dma, dma,
        ],
        compiler_params=pltpu.CompilerParams(
            collective_id=0, has_side_effects=True, vmem_limit_bytes=VMEM_BYTES
        ),
        name="network",
    )(counts, offsets, image, own_target, cut_target, *weights)


def sum_kernel(p_ref, full, from_core, held_core, from_xy, from_z, held_z, send, recv):
    ty = lax.axis_index("ty")
    tx = lax.axis_index("tx")
    core = ty % 2
    x = (ty // 2) % 4
    z = (tx // 4) * 2 + ty // 8
    y = tx % 4
    xy = y * 4 + x

    def device(core_at, xy_at, z_at):
        return ((z_at % 2) * 8 + (xy_at % 4) * 2 + core_at, (z_at // 2) * 4 + xy_at // 4)

    def core_peer():
        return device(1 - core, xy, z)

    def xy_peer(d):
        return ((y + d // 4) % 4) * 4 + (x + d % 4) % 4

    def z_peer(d):
        return device(core, xy, (z + d) % 8)

    barrier = pltpu.get_barrier_semaphore()
    pl.semaphore_signal(barrier, inc=1, device_id=core_peer(), device_id_type=MESH)
    for d in range(1, 16):
        pl.semaphore_signal(barrier, inc=1, device_id=device(core, xy_peer(d), z), device_id_type=MESH)
    for d in range(1, 8):
        pl.semaphore_signal(barrier, inc=1, device_id=z_peer(d), device_id_type=MESH)
    pl.semaphore_wait(barrier, 23)

    counter = [0]

    def push(src, dst, peer):
        copy = pltpu.make_async_remote_copy(
            src_ref=src, dst_ref=dst, send_sem=send.at[counter[0]], recv_sem=recv.at[counter[0]],
            device_id=peer, device_id_type=MESH)
        counter[0] += 1
        copy.start()
        return copy

    def finish(copies):
        for copy in copies:
            copy.wait()

    def rows(at, count):
        return pl.ds(pl.multiple_of(at, 16), count)

    far_first = (10, 2, 8, 6, 9, 11, 14, 1, 3, 4, 12, 5, 7, 13, 15)
    finish([push(p_ref.at[rows((1 - core) * 768, 768)], from_core, core_peer())])
    held_core[...] = p_ref[rows(core * 768, 768), :] + from_core[...]
    finish([push(held_core.at[rows(xy_peer(d) * 48, 48)], from_xy.at[d - 1], device(core, xy_peer(d), z))
            for d in far_first])
    total = held_core[rows(xy * 48, 48), :]
    for d in range(15):
        total = total + from_xy[d]
    held_z[...] = total
    from_z[z] = total
    finish([push(held_z, from_z.at[z], z_peer(d)) for d in (4, 3, 5, 2, 6, 1, 7)])
    total = from_z[0]
    for d in range(1, 8):
        total = total + from_z[d]
    at_xy = core * 768 + xy * 48
    full[rows(at_xy, 48), :] = total
    mine = full.at[rows(at_xy, 48)]
    finish([push(mine, mine, device(core, xy_peer(d), z)) for d in far_first])
    mine = full.at[rows(core * 768, 768)]
    finish([push(mine, mine, core_peer())])


def sum_everywhere(packed):
    vmem = pl.BlockSpec(memory_space=pltpu.VMEM)
    return pl.pallas_call(
        sum_kernel,
        out_shape=jax.ShapeDtypeStruct((ROWS, 128), F32),
        in_specs=[vmem],
        out_specs=vmem,
        scratch_shapes=[
            pltpu.VMEM((768, 128), F32),
            pltpu.VMEM((768, 128), F32),
            pltpu.VMEM((15, 48, 128), F32),
            pltpu.VMEM((8, 48, 128), F32),
            pltpu.VMEM((48, 128), F32),
            pltpu.SemaphoreType.DMA((39,)),
            pltpu.SemaphoreType.DMA((39,)),
        ],
        compiler_params=pltpu.CompilerParams(
            collective_id=1, has_side_effects=True, vmem_limit_bytes=VMEM_BYTES
        ),
        name="sums",
    )(packed)


def unpack_kernel(full, shown, o1_ref, o2_ref, o3_ref, oh_ref, cut_pred_ref):
    o3_ref[:, :128] = full[0:512, :]
    o3_ref[:, 128:] = full[512:1024, :]
    o2_ref[...] = full[1024:1280, :]
    o1_ref[...] = full[1280:1304, :64]
    oh_ref[:, :128] = full[1304:1312, :]
    oh_ref[:, 128:] = full[1312:1320, :]
    cut_pred_ref[...] = shown[...]


def unpack(full, shown):
    vmem = pl.BlockSpec(memory_space=pltpu.VMEM)
    return pl.pallas_call(
        unpack_kernel,
        out_shape=(
            jax.ShapeDtypeStruct((24, 64), F32),
            jax.ShapeDtypeStruct((256, 128), F32),
            jax.ShapeDtypeStruct((512, 256), F32),
            jax.ShapeDtypeStruct((8, 256), F32),
            jax.ShapeDtypeStruct((8, 1024), BF),
        ),
        in_specs=[vmem, vmem],
        out_specs=(vmem,) * 5,
        name="unpack",
    )(full, shown)


def per_device(sky_tile, request_offset, request_count, tile_target, cut_target, w_first, w_second, w_third, w_head):
    packed, cut_pred = network(
        request_count.reshape(-1), request_offset.transpose(0, 1, 3, 4, 2), sky_tile,
        tile_target[0, 0], cut_target[0, 0], (w_first, w_second, w_third, w_head))
    *sums, shown = unpack(sum_everywhere(packed), cut_pred)
    return (*sums, shown[None, None])


def solution(mesh):
    return jax.shard_map(
        per_device,
        mesh=mesh,
        in_specs=(
            P(None, "ty", "tx"),
            P("ty", "tx", None, None, None),
            P("ty", "tx", None),
            P("ty", "tx", None, None),
            P("ty", "tx", None, None),
            P(),
            P(),
            P(),
            P(),
        ),
        out_specs=(P(), P(), P(), P(), P("ty", "tx", None, None)),
        check_vma=False,
    )
```

time: 93.8 us -> 77.3 us (0.82)
  Pallas kernels: 86.2 us -> 76.5 us
  local copies, waits for them, and re-layouts: 6.73 us -> 0 us
    pallas_call x2, Pallas kernels: 71.8 us -> 35.7 us  [the longest x1 33.7 us: sum_everywhere(): pl.pallas_call(sum_kernel, out_shape=jax.ShapeDtypeStruct((ROWS, 128), F3...]
    pallas_call x1, Pallas kernels: 14.3 us -> 40.8 us  [network(): pl.pallas_call(net_kernel, out_shape=(jax.ShapeDtypeStruct((ROWS, 128), F...]
    unnamed x9 -> x0, local copies, waits for them, and re-layouts: 6.12 us -> none
where the time goes in v2:
time: 77.3 us; the launch traced here: 77.2 us
  Pallas kernels  76.5 us (99%)
    pallas_call x1, Pallas kernels, network(): pl.pallas_call(net_kernel, out_shape=(jax.ShapeDtypeStruct((ROWS, 128), F...  40.8 us
    pallas_call x1, Pallas kernels, sum_everywhere(): pl.pallas_call(sum_kernel, out_shape=jax.ShapeDtypeStruct((ROWS, 128), F3...  33.7 us
    pallas_call x1, Pallas kernels, unpack(): pl.pallas_call(unpack_kernel, out_shape=(jax.ShapeDtypeStruct((24, 64), F...  1.99 us

profile of v2, /device:TPU:1, one launch (start us, length us, event | category | flops | bytes accessed | tf_op | source)
XLA Modules:
  0.0 77.2 jit_solution(3137432102940918912)
XLA Ops:
  0.6 40.8 %network.1 = (f32[1536,128]{1,0:T(8,128)}, bf16[8,1024]{1,0:T(8,128)(2,1)}) custom-call(s32[8]{0:T(128)} %bitcast.8, s32[1,1,2,2,8]{4,3,2,1,0:T(2,128)} %bitcast.7, bf16[6,128,256]{2,1,0:T(8,128)(2,1)} %img_ref.1, f32[8,512]{1,0:T(8,128)} %bitcast.6, f32[8,1024]{1,0:T(8,128)} %bitcast.5, bf16[24,64]{1,0:T(8,128)(2,1)} %w1_ref.1, bf16[256,128]{1,0:T(8,128)(2,1)} %w2_ref.1, ...), custom_call_target="tpu_custom_call" | custom-call | tf_op jit(solution)/shard_map/network/pallas_call | solution.py:261
  41.4 33.7 %sums.1.full = f32[1536,128]{1,0:T(8,128)} custom-call(f32[1536,128]{1,0:T(8,128)} %get-tuple-element.12.p_ref), custom_call_target="tpu_custom_call" | custom-call | tf_op jit(solution)/shard_map/sums/pallas_call | solution.py:372
  75.2 2.0 %unpack.1 = (f32[24,64]{1,0:T(8,128)}, f32[256,128]{1,0:T(8,128)}, f32[512,256]{1,0:T(8,128)}, f32[8,256]{1,0:T(8,128)}, bf16[8,1024]{1,0:T(8,128)(2,1)}) custom-call(f32[1536,128]{1,0:T(8,128)} %sums.1.full, bf16[8,1024]{1,0:T(8,128)(2,1)} %get-tuple-element.13.shown), custom_call_target="tpu_custom_call" | custom-call | tf_op jit(solution)/shard_map/unpack/pallas_call | solution.py:405

commit v3 on v2

v3 whole, which is shorter than its diff:
```python
import functools

import jax
import jax.numpy as jnp
from jax import lax
from jax.experimental import pallas as pl
from jax.experimental.pallas import tpu as pltpu
from jax.sharding import PartitionSpec as P

DIRECTIONS = ((-1, -1), (-1, 0), (-1, 1), (0, -1), (0, 1), (1, -1), (1, 0), (1, 1))
MESH = pl.DeviceIdType.MESH
BF = jnp.bfloat16
F32 = jnp.float32
I32 = jnp.int32
VMEM_BYTES = 56 * 1024 * 1024
ROWS = 1536


def iota(shape, dim):
    return lax.broadcasted_iota(I32, shape, dim)


def one_hot(condition, kind=BF):
    return jnp.where(condition, 1.0, 0.0).astype(kind)


def nn(a, b):
    return lax.dot_general(a, b, (((1,), (0,)), ((), ())), preferred_element_type=F32)


def nt(a, b):
    return lax.dot_general(a, b, (((1,), (1,)), ((), ())), preferred_element_type=F32)


def tn(a, b):
    return lax.dot_general(a, b, (((0,), (0,)), ((), ())), preferred_element_type=F32)


def first_mask():
    row = iota((512, 192), 0)
    col = iota((512, 192), 1)
    return ((row >> 7) == ((col & 7) >> 1)) & (((row >> 6) & 1) == jnp.where(col < 96, 0, 1))


def first_spread():
    row = iota((24, 192), 0)
    col = iota((24, 192), 1)
    return row == ((col % 48) // 8) * 4 + (col & 1) * 2 + ((col // 48) & 1)


def silu(pre):
    sig = 0.5 * jnp.tanh(0.5 * pre) + 0.5
    act = pre * sig
    return act.astype(BF), sig + act * (1.0 - sig)


def pick(flag, yes, no):
    return jnp.where(flag, jnp.int32(yes), jnp.int32(no))


def step_of(k):
    at = k + jnp.where(k >= 4, 1, 0)
    return at // 3 - 1, at % 3 - 1


def net_kernel(cnt_ref, off_ref, img_hbm, own_target_hbm, cut_target_hbm, w1_hbm, w2_hbm, w3_hbm, wh_hbm,
               full, cut_pred_ref,
               img_ref, own_target_ref, cut_target_ref, w1_ref, w2_ref, w3_ref, wh_ref,
               msg, req, rows_sel, rows_got, cut, got,
               field, place_own, place_cut, wide1, w2, w2t, w3, w3t,
               act1, slope1, act2, slope2, delta1, delta2,
               target, mask, g1, g2, g3, gh,
               parts_a, from_core_a, held_core_a, from_xy_a, held_z_a, from_z_a,
               parts_b, from_core_b, held_core_b, from_xy_b, held_z_b, from_z_b,
               fetch, req_send, req_recv, rep_send, rep_recv, sum_send, sum_recv):
    ty = lax.axis_index("ty")
    tx = lax.axis_index("tx")
    n_ty = lax.axis_size("ty")
    n_tx = lax.axis_size("tx")
    core = ty % 2
    x = (ty // 2) % 4
    y = tx % 4
    z = (tx // 4) * 2 + ty // 8
    xy = y * 4 + x
    upper = y >= 2

    def device(dy, dx):
        return (lax.rem(ty + dy + n_ty, n_ty), lax.rem(tx + dx + n_tx, n_tx))

    def place_of(core_at, xy_at, z_at):
        return ((z_at % 2) * 8 + (xy_at % 4) * 2 + core_at, (z_at // 2) * 4 + xy_at // 4)

    def xy_peer(d):
        return ((y + d // 4) % 4) * 4 + (x + d % 4) % 4

    core_peer = place_of(1 - core, xy, z)

    def z_peer(d):
        return place_of(core, xy, (z + d) % 8)

    barrier = pltpu.get_barrier_semaphore()
    greeted = [device(dy, dx) for dy, dx in DIRECTIONS] + [core_peer]
    greeted += [z_peer(d) for d in range(1, 8)]
    greeted += [place_of(core, xy_peer(d), z) for d in range(1, 16)]
    for peer in greeted:
        pl.semaphore_signal(barrier, inc=1, device_id=peer, device_id_type=MESH)

    fetched = []
    for at, (src, dst) in enumerate((
            (img_hbm, img_ref), (w1_hbm, w1_ref), (w2_hbm, w2_ref), (w3_hbm, w3_ref), (wh_hbm, wh_ref),
            (own_target_hbm, own_target_ref), (cut_target_hbm, cut_target_ref))):
        copy = pltpu.make_async_copy(src, dst, fetch.at[at])
        copy.start()
        fetched.append(copy)

    lane = iota((8, 128), 1)
    sub = iota((8, 128), 0)
    first = lane < 64
    col_step = 8 * (lane & 7) + ((lane >> 3) & 7)
    row_step = lane & 63

    def offset(coord, p, k):
        return jnp.broadcast_to(off_ref[0, 0, coord, p:p + 1, k:k + 1], (8, 128))

    for k in range(8):
        r0 = jnp.where(first, offset(0, 0, k), offset(0, 1, k))
        c0 = jnp.where(first, offset(1, 0, k), offset(1, 1, k) + 256)
        msg[k] = jnp.where(sub == 0, c0 + col_step, r0 + row_step)

    pl.semaphore_wait(barrier, len(greeted))

    requests = []
    for k, (dy, dx) in enumerate(DIRECTIONS):
        copy = pltpu.make_async_remote_copy(
            src_ref=msg.at[k], dst_ref=req.at[k],
            send_sem=req_send.at[k], recv_sem=req_recv.at[k],
            device_id=device(dy, dx), device_id_type=MESH,
        )
        copy.start()
        requests.append(copy)

    lanes = iota((1024, 128), 1)
    src = iota((1024, 128), 0)
    goal = (src & 7) * 128 + (src >> 8) * 32 + ((src & 255) >> 3)
    for j in range(8):
        place_own[:, j * 128:(j + 1) * 128] = one_hot(lanes + j * 128 == goal)
    src = iota((1024, 128), 0)
    goal = ((src >> 3) & 7) * 128 + ((src >> 6) & 1) * 64 + (src >> 7) * 8 + (src & 7)
    for j in range(8):
        place_cut[:, j * 128:(j + 1) * 128] = one_hot(lanes + j * 128 == goal)

    fetched[0].wait()
    for copy in requests:
        copy.wait()

    def reply(k):
        dy, dx = step_of(k)
        return pltpu.make_async_remote_copy(
            src_ref=cut.at[k], dst_ref=got.at[k],
            send_sem=rep_send.at[k], recv_sem=rep_recv.at[k],
            device_id=device(-dy, -dx), device_id_type=MESH,
        )

    for group in (((0, 2), (3, 4), (5, 7)), ((2, 0), (4, 3), (7, 5), (1, 1), (6, 6))):
        slots = [pick(upper, *pair) for pair in group]
        wide_rows = 128 * len(slots)
        for at, k in enumerate(slots):
            rows_sel[:, at * 128:(at + 1) * 128] = one_hot(iota((128, 128), 0) == req[k][1:2, :])
        for band in range(6):
            rows_got[band, :wide_rows] = tn(rows_sel[:, :wide_rows], img_ref[band])
        for at, k in enumerate(slots):
            halves = []
            for p in range(2):
                pieces = []
                for block in range(8):
                    row = at * 128 + p * 64 + block * 8
                    for band in range(6):
                        pieces.append(rows_got[band, row:row + 8, :])
                halves.append(jnp.concatenate(pieces, axis=0).astype(BF))
            cols_sel = one_hot(iota((512, 128), 0) == req[k][0:1, :])
            cut[k] = (nn(halves[0], cols_sel[:256]) + nn(halves[1], cols_sel[256:])).astype(BF)
            reply(k).start()

    for copy in fetched[1:]:
        copy.wait()

    up = one_hot((iota((512, 64), 0) & 63) == iota((512, 64), 1))
    wide = nn(nt(up, w1_ref[...]).astype(BF), one_hot(first_spread()))
    wide1[...] = jnp.where(first_mask(), wide, 0.0).astype(BF)
    new = iota((256, 256), 0)
    w2[...] = nn(one_hot(iota((256, 256), 1) == (new & 63) * 4 + (new >> 6)), w2_ref[...]).astype(BF)
    new = iota((256, 256), 1)
    w2t[...] = tn(w2_ref[...], one_hot(iota((256, 256), 0) == (new & 63) * 4 + (new >> 6))).astype(BF)
    new = iota((512, 512), 0)
    w3[...] = nn(one_hot(iota((512, 512), 1) == (new & 127) * 4 + (new >> 7)), w3_ref[...]).astype(BF)
    new = iota((512, 512), 1)
    w3t[...] = tn(w3_ref[...], one_hot(iota((512, 512), 0) == (new & 127) * 4 + (new >> 7))).astype(BF)
    wh = wh_ref[...]

    lines = []
    images = [img_ref[band].astype(F32) for band in range(6)]
    for q in range(4):
        for band in range(6):
            lines.append(jnp.concatenate(
                [images[band][(4 * q + r) * 8:(4 * q + r) * 8 + 8] for r in range(4)], axis=1))
    spread = nn(jnp.concatenate(lines, axis=0).astype(BF), place_own[...]).astype(BF)
    for q in range(4):
        for j in range(8):
            field[j // 4, (j % 4) * 48:(j % 4) * 48 + 48, q * 128:(q + 1) * 128] = (
                spread[q * 48:(q + 1) * 48, j * 128:(j + 1) * 128])

    target[...] = own_target_ref[...]
    mask[...] = jnp.full((8, 512), 1.0, F32)
    g1[...] = jnp.zeros_like(g1)
    g2[...] = jnp.zeros_like(g2)
    g3[...] = jnp.zeros_like(g3)
    gh[...] = jnp.zeros_like(gh)

    def slot_of(step, at):
        early = pick(upper, (0, 3, 5, 1)[at], (2, 4, 7, 1)[at])
        late = pick(upper, (6, 2, 4, 7)[at], (6, 0, 3, 5)[at])
        return jnp.where(step == 1, early, late)

    def take(step):
        stack = []
        for at in range(4):
            k = slot_of(step, at)
            reply(k).wait_recv()
            stack.append(jnp.concatenate([got[k, r * 48:(r + 1) * 48, :] for r in range(8)], axis=1))
            here = slice(at * 128, at * 128 + 128)
            target[:, here] = cut_target_ref[:, pl.ds(pl.multiple_of(k * 128, 128), 128)]
            mask[:, here] = jnp.where((iota((8, 128), 1) >> 6) < cnt_ref[k], 1.0, 0.0)
        spread = nn(jnp.concatenate(stack, axis=0), place_cut[...]).astype(BF)
        for at in range(4):
            for j in range(8):
                field[j // 4, (j % 4) * 48:(j % 4) * 48 + 48, at * 128:(at + 1) * 128] = (
                    spread[at * 48:(at + 1) * 48, j * 128:(j + 1) * 128])

    def show(step, pred):
        shown = (pred * mask[...]).astype(BF)
        for at in range(4):
            k = slot_of(step, at)
            cut_pred_ref[:, pl.ds(pl.multiple_of(k * 128, 128), 128)] = shown[:, at * 128:at * 128 + 128]

    def upward():
        for ac in range(2):
            act1[ac], slope1[ac] = silu(nn(wide1[...], field[ac]))
            for ar in range(2):
                at = (ar * 2 + ac) * 128
                act2[at:at + 128], slope2[at:at + 128] = silu(nn(w2t[...], act1[ac, ar * 256:ar * 256 + 256]))
        act3, slope3 = silu(nn(w3t[...], act2[...]))
        pred = nn(wh, act3)
        grad = ((pred - target[...]) * mask[...] * (1.0 / 256.0)).astype(BF)
        gh[...] += nt(grad, act3)
        delta3 = (tn(wh, grad) * slope3).astype(BF)
        g3[...] += nt(act2[...], delta3)
        return pred, delta3

    def back_third(delta3):
        delta2[...] = (nn(w3[...], delta3) * slope2[...]).astype(BF)

    def back_second(ac):
        for ar in range(2):
            at = (ar * 2 + ac) * 128
            rows = slice(ar * 256, ar * 256 + 256)
            g2[...] += nt(act1[ac, rows], delta2[at:at + 128])
            delta1[ac, rows] = (nn(w2[...], delta2[at:at + 128]) * slope1[ac, rows]).astype(BF)
        g1[...] += nt(delta1[ac], field[ac])

    def part(step, carry):
        @pl.when(step > 0)
        def cutouts():
            take(step)

        pred, delta3 = upward()

        @pl.when(step > 0)
        def predictions():
            show(step, pred)

        back_third(delta3)
        for ac in range(2):
            back_second(ac)
        return carry

    lax.fori_loop(0, 2, part, 0)

    used = [0]

    def push(src, dst, peer):
        copy = pltpu.make_async_remote_copy(
            src_ref=src, dst_ref=dst, send_sem=sum_send.at[used[0]], recv_sem=sum_recv.at[used[0]],
            device_id=peer, device_id_type=MESH)
        used[0] += 1
        copy.start()
        return copy

    def finish(copies):
        for copy in copies:
            copy.wait()

    def rows(at, count):
        return pl.ds(pl.multiple_of(at, 8), count)

    far_first = (10, 2, 8, 6, 9, 11, 14, 1, 3, 4, 12, 5, 7, 13, 15)
    far_z = (4, 3, 5, 2, 6, 1, 7)

    class Stream:
        def __init__(self, base, piece, parts, from_core, held_core, from_xy, held_z, from_z):
            self.base, self.piece, self.half = base, piece, piece * 16
            self.parts, self.from_core, self.held_core = parts, from_core, held_core
            self.from_xy, self.held_z, self.from_z = from_xy, held_z, from_z

        def send_core(self):
            self.going = [push(self.parts.at[rows((1 - core) * self.half, self.half)], self.from_core, core_peer)]

        def send_plane(self):
            finish(self.going)
            self.held_core[...] = self.parts[rows(core * self.half, self.half), :] + self.from_core[...]
            self.going = [
                push(self.held_core.at[rows(xy_peer(d) * self.piece, self.piece)], self.from_xy.at[d - 1],
                     place_of(core, xy_peer(d), z)) for d in far_first]

        def send_z(self):
            finish(self.going)
            total = self.held_core[rows(xy * self.piece, self.piece), :]
            for d in range(15):
                total = total + self.from_xy[d]
            self.held_z[...] = total
            self.from_z[z] = total
            self.going = [push(self.held_z, self.from_z.at[z], z_peer(d)) for d in far_z]

        def gather_plane(self):
            finish(self.going)
            total = self.from_z[0]
            for d in range(1, 8):
                total = total + self.from_z[d]
            at = self.base + core * self.half + xy * self.piece
            full[rows(at, self.piece), :] = total
            mine = full.at[rows(at, self.piece)]
            self.going = [push(mine, mine, place_of(core, xy_peer(d), z)) for d in far_first]

        def gather_core(self):
            finish(self.going)
            mine = full.at[rows(self.base + core * self.half, self.half)]
            self.going = [push(mine, mine, core_peer)]

        def end(self):
            finish(self.going)

    third = Stream(0, 32, parts_a, from_core_a, held_core_a, from_xy_a, held_z_a, from_z_a)
    others = Stream(1024, 16, parts_b, from_core_b, held_core_b, from_xy_b, held_z_b, from_z_b)

    take(2)
    pred, delta3 = upward()
    for phase in range(4):
        for half in range(2):
            parts_a[pl.ds(half * 512 + phase, 128, stride=4), :] = (
                g3[phase * 128:phase * 128 + 128, half * 128:half * 128 + 128])
    third.send_core()
    show(2, pred)
    back_third(delta3)
    back_second(0)
    third.send_plane()
    back_second(1)
    for phase in range(4):
        parts_b[pl.ds(phase, 64, stride=4), :] = g2[phase * 64:phase * 64 + 64, :]
    picked = jnp.where(first_mask(), g1[...], 0.0)
    folded = lax.dot_general(
        one_hot(first_spread(), F32), picked, (((1,), (1,)), ((), ())),
        precision=lax.Precision.HIGHEST, preferred_element_type=F32)
    parts_b[256:280, :] = lax.dot_general(
        folded, one_hot((iota((512, 128), 0) & 63) == iota((512, 128), 1), F32), (((1,), (0,)), ((), ())),
        precision=lax.Precision.HIGHEST, preferred_element_type=F32)
    parts_b[280:288, :] = gh[:, :128]
    parts_b[288:296, :] = gh[:, 128:]
    parts_b[296:, :] = jnp.zeros((216, 128), F32)
    others.send_core()
    third.send_z()
    others.send_plane()
    third.gather_plane()
    others.send_z()
    third.gather_core()
    others.gather_plane()
    others.gather_core()
    third.end()
    others.end()
    for k in range(8):
        reply(jnp.int32(k)).wait_send()


def network(counts, offsets, image, own_target, cut_target, weights):
    vmem = pl.BlockSpec(memory_space=pltpu.VMEM)
    dma = pltpu.SemaphoreType.DMA((8,))
    return pl.pallas_call(
        net_kernel,
        out_shape=(jax.ShapeDtypeStruct((ROWS, 128), F32), jax.ShapeDtypeStruct((8, 1024), BF)),
        in_specs=[pl.BlockSpec(memory_space=pltpu.SMEM), vmem] + [pl.BlockSpec(memory_space=pl.ANY)] * 7,
        out_specs=(vmem, vmem),
        scratch_shapes=[
            pltpu.VMEM((6, 128, 256), BF),
            pltpu.VMEM((8, 512), F32),
            pltpu.VMEM((8, 1024), F32),
            pltpu.VMEM((24, 64), BF),
            pltpu.VMEM((256, 128), BF),
            pltpu.VMEM((512, 256), BF),
            pltpu.VMEM((8, 256), BF),
            pltpu.VMEM((8, 8, 128), I32),
            pltpu.VMEM((8, 8, 128), I32),
            pltpu.VMEM((128, 640), BF),
            pltpu.VMEM((6, 640, 256), F32),
            pltpu.VMEM((8, 384, 128), BF),
            pltpu.VMEM((8, 384, 128), BF),
            pltpu.VMEM((2, 192, 512), BF),
            pltpu.VMEM((1024, 1024), BF),
            pltpu.VMEM((1024, 1024), BF),
            pltpu.VMEM((512, 192), BF),
            pltpu.VMEM((256, 128), BF),
            pltpu.VMEM((128, 256), BF),
            pltpu.VMEM((512, 256), BF),
            pltpu.VMEM((256, 512), BF),
            pltpu.VMEM((2, 512, 512), BF),
            pltpu.VMEM((2, 512, 512), F32),
            pltpu.VMEM((512, 512), BF),
            pltpu.VMEM((512, 512), F32),
            pltpu.VMEM((2, 512, 512), BF),
            pltpu.VMEM((512, 512), BF),
            pltpu.VMEM((8, 512), F32),
            pltpu.VMEM((8, 512), F32),
            pltpu.VMEM((512, 192), F32),
            pltpu.VMEM((256, 128), F32),
            pltpu.VMEM((512, 256), F32),
            pltpu.VMEM((8, 256), F32),
            pltpu.VMEM((1024, 128), F32),
            pltpu.VMEM((512, 128), F32),
            pltpu.VMEM((512, 128), F32),
            pltpu.VMEM((15, 32, 128), F32),
            pltpu.VMEM((32, 128), F32),
            pltpu.VMEM((8, 32, 128), F32),
            pltpu.VMEM((512, 128), F32),
            pltpu.VMEM((256, 128), F32),
            pltpu.VMEM((256, 128), F32),
            pltpu.VMEM((15, 16, 128), F32),
            pltpu.VMEM((16, 128), F32),
            pltpu.VMEM((8, 16, 128), F32),
            dma, dma, dma, dma, dma,
            pltpu.SemaphoreType.DMA((78,)),
            pltpu.SemaphoreType.DMA((78,)),
        ],
        compiler_params=pltpu.CompilerParams(
            collective_id=0, has_side_effects=True, vmem_limit_bytes=VMEM_BYTES
        ),
        name="network",
    )(counts, offsets, image, own_target, cut_target, *weights)


def unpack_kernel(full, shown, o1_ref, o2_ref, o3_ref, oh_ref, cut_pred_ref):
    o3_ref[:, :128] = full[0:512, :]
    o3_ref[:, 128:] = full[512:1024, :]
    o2_ref[...] = full[1024:1280, :]
    o1_ref[...] = full[1280:1304, :64]
    oh_ref[:, :128] = full[1304:1312, :]
    oh_ref[:, 128:] = full[1312:1320, :]
    cut_pred_ref[...] = shown[...]


def unpack(full, shown):
    vmem = pl.BlockSpec(memory_space=pltpu.VMEM)
    return pl.pallas_call(
        unpack_kernel,
        out_shape=(
            jax.ShapeDtypeStruct((24, 64), F32),
            jax.ShapeDtypeStruct((256, 128), F32),
            jax.ShapeDtypeStruct((512, 256), F32),
            jax.ShapeDtypeStruct((8, 256), F32),
            jax.ShapeDtypeStruct((8, 1024), BF),
        ),
        in_specs=[vmem, vmem],
        out_specs=(vmem,) * 5,
        name="unpack",
    )(full, shown)


def per_device(sky_tile, request_offset, request_count, tile_target, cut_target, w_first, w_second, w_third, w_head):
    full, cut_pred = network(
        request_count.reshape(-1), request_offset.transpose(0, 1, 3, 4, 2), sky_tile,
        tile_target[0, 0], cut_target[0, 0], (w_first, w_second, w_third, w_head))
    *sums, shown = unpack(full, cut_pred)
    return (*sums, shown[None, None])


def solution(mesh):
    return jax.shard_map(
        per_device,
        mesh=mesh,
        in_specs=(
            P(None, "ty", "tx"),
            P("ty", "tx", None, None, None),
            P("ty", "tx", None),
            P("ty", "tx", None, None),
            P("ty", "tx", None, None),
            P(),
            P(),
            P(),
            P(),
        ),
        out_specs=(P(), P(), P(), P(), P("ty", "tx", None, None)),
        check_vma=False,
    )
```

time: 77.3 us -> 71.5 us (0.925)
  Pallas kernels: 76.5 us -> 70.7 us
    pallas_call x1 -> x0, Pallas kernels: 33.7 us -> none  [sum_everywhere(): pl.pallas_call(sum_kernel, out_shape=jax.ShapeDtypeStruct((ROWS, 128), F3...]
    pallas_call x1, Pallas kernels: 40.8 us -> 68.7 us  [network(): pl.pallas_call(net_kernel, out_shape=(jax.ShapeDtypeStruct((ROWS, 128), F...]
where the time goes in v3:
time: 71.5 us; the launch traced here: 71.3 us
  Pallas kernels  70.7 us (99%)
    pallas_call x1, Pallas kernels, network(): pl.pallas_call(net_kernel, out_shape=(jax.ShapeDtypeStruct((ROWS, 128), F...  68.7 us
    pallas_call x1, Pallas kernels, unpack(): pl.pallas_call(unpack_kernel, out_shape=(jax.ShapeDtypeStruct((24, 64), F...  1.99 us

profile of v3, /device:TPU:1, one launch (start us, length us, event | category | flops | bytes accessed | tf_op | source)
XLA Modules:
  0.0 71.3 jit_solution(814488360530919898)
XLA Ops:
  0.6 68.7 %network.1 = (f32[1536,128]{1,0:T(8,128)}, bf16[8,1024]{1,0:T(8,128)(2,1)}) custom-call(s32[8]{0:T(128)} %bitcast.8, s32[1,1,2,2,8]{4,3,2,1,0:T(2,128)} %bitcast.7, bf16[6,128,256]{2,1,0:T(8,128)(2,1)} %img_hbm.1, f32[8,512]{1,0:T(8,128)} %bitcast.6, f32[8,1024]{1,0:T(8,128)} %bitcast.5, bf16[24,64]{1,0:T(8,128)(2,1)} %w1_hbm.1, bf16[256,128]{1,0:T(8,128)(2,1)} %w2_hbm.1, ...), custom_call_target="tpu_custom_call" | custom-call | tf_op jit(solution)/shard_map/network/pallas_call | solution.py:395
  69.3 2.0 %unpack.1 = (f32[24,64]{1,0:T(8,128)}, f32[256,128]{1,0:T(8,128)}, f32[512,256]{1,0:T(8,128)}, f32[8,256]{1,0:T(8,128)}, bf16[8,1024]{1,0:T(8,128)(2,1)}) custom-call(f32[1536,128]{1,0:T(8,128)} %get-tuple-element.12.full, bf16[8,1024]{1,0:T(8,128)(2,1)} %get-tuple-element.13.shown), custom_call_target="tpu_custom_call" | custom-call | tf_op jit(solution)/shard_map/unpack/pallas_call | solution.py:469

commit v4 on v3

--- a/solution.py
+++ b/solution.py
@@ -66,13 +66,13 @@
 def net_kernel(cnt_ref, off_ref, img_hbm, own_target_hbm, cut_target_hbm, w1_hbm, w2_hbm, w3_hbm, wh_hbm,
                full, cut_pred_ref,
                img_ref, own_target_ref, cut_target_ref, w1_ref, w2_ref, w3_ref, wh_ref,
-               msg, req, rows_sel, rows_got, cut, got,
+               msg, req, rows_sel, rows_got, cut, got, passing,
                field, place_own, place_cut, wide1, w2, w2t, w3, w3t,
                act1, slope1, act2, slope2, delta1, delta2,
                target, mask, g1, g2, g3, gh,
                parts_a, from_core_a, held_core_a, from_xy_a, held_z_a, from_z_a,
                parts_b, from_core_b, held_core_b, from_xy_b, held_z_b, from_z_b,
-               fetch, req_send, req_recv, rep_send, rep_recv, sum_send, sum_recv):
+               fetch, req_send, req_recv, rep_send, rep_recv, pass_sem, sum_send, sum_recv):
     ty = lax.axis_index("ty")
     tx = lax.axis_index("tx")
     n_ty = lax.axis_size("ty")
@@ -159,6 +159,27 @@
             src_ref=cut.at[k], dst_ref=got.at[k],
             send_sem=rep_send.at[k], recv_sem=rep_recv.at[k],
             device_id=device(-dy, -dx), device_id_type=MESH,
+        )
+
+    at_edge = (y == 0) | (y == 3)
+    relayed = ((3, 4), (0, 2))
+    by_relay = (at_edge, at_edge & (core == 0))
+    relay_tx = lax.rem(tx + pick(y == 3, 13, 3), 16)
+    onward_tx = lax.rem(tx + pick(y == 3, 12, 4), 16)
+
+    def to_relay(which):
+        return pltpu.make_async_remote_copy(
+            src_ref=cut.at[pick(y == 3, *relayed[which])], dst_ref=passing.at[which],
+            send_sem=pass_sem.at[which], recv_sem=pass_sem.at[2 + which],
+            device_id=(ty, relay_tx), device_id_type=MESH,
+        )
+
+    def onward(which):
+        slot = pick(y == 0, *relayed[which])
+        return pltpu.make_async_remote_copy(
+            src_ref=passing.at[which], dst_ref=got.at[slot],
+            send_sem=pass_sem.at[4 + which], recv_sem=rep_recv.at[slot],
+            device_id=(lax.rem(ty + which, n_ty), onward_tx), device_id_type=MESH,
         )
 
     for group in (((0, 2), (3, 4), (5, 7)), ((2, 0), (4, 3), (7, 5), (1, 1), (6, 6))):
@@ -179,7 +200,19 @@
                 halves.append(jnp.concatenate(pieces, axis=0).astype(BF))
             cols_sel = one_hot(iota((512, 128), 0) == req[k][0:1, :])
             cut[k] = (nn(halves[0], cols_sel[:256]) + nn(halves[1], cols_sel[256:])).astype(BF)
-            reply(k).start()
+            if group[at] not in relayed:
+                reply(k).start()
+                continue
+
+            which = relayed.index(group[at])
+
+            @pl.when(by_relay[which])
+            def first_leg():
+                to_relay(which).start()
+
+            @pl.when(jnp.logical_not(by_relay[which]))
+            def straight():
+                reply(k).start()
 
     for copy in fetched[1:]:
         copy.wait()
@@ -270,6 +303,12 @@
     def part(step, carry):
         @pl.when(step > 0)
         def cutouts():
+            for which in range(2):
+                @pl.when(by_relay[which])
+                def pass_on():
+                    to_relay(which).wait_recv()
+                    onward(which).start()
+
             take(step)
 
         pred, delta3 = upward()
@@ -376,17 +415,30 @@
     parts_b[288:296, :] = gh[:, 128:]
     parts_b[296:, :] = jnp.zeros((216, 128), F32)
     others.send_core()
+    others.send_plane()
     third.send_z()
-    others.send_plane()
+    others.send_z()
     third.gather_plane()
-    others.send_z()
+    others.gather_plane()
     third.gather_core()
-    others.gather_plane()
     others.gather_core()
     third.end()
     others.end()
+    for which in range(2):
+        @pl.when(by_relay[which])
+        def passed():
+            to_relay(which).wait_send()
+            onward(which).wait_send()
+
     for k in range(8):
-        reply(jnp.int32(k)).wait_send()
+        straight = jnp.bool_(True)
+        for which in range(2):
+            if k in relayed[which]:
+                straight = jnp.logical_not(by_relay[which] & (pick(y == 3, *relayed[which]) == k))
+
+        @pl.when(straight)
+        def answered():
+            reply(jnp.int32(k)).wait_send()
 
 
 def network(counts, offsets, image, own_target, cut_target, weights):
@@ -411,6 +463,7 @@
             pltpu.VMEM((6, 640, 256), F32),
             pltpu.VMEM((8, 384, 128), BF),
             pltpu.VMEM((8, 384, 128), BF),
+            pltpu.VMEM((2, 384, 128), BF),
             pltpu.VMEM((2, 192, 512), BF),
             pltpu.VMEM((1024, 1024), BF),
             pltpu.VMEM((1024, 1024), BF),
@@ -444,6 +497,7 @@
             pltpu.VMEM((16, 128), F32),
             pltpu.VMEM((8, 16, 128), F32),
             dma, dma, dma, dma, dma,
+            pltpu.SemaphoreType.DMA((6,)),
             pltpu.SemaphoreType.DMA((78,)),
             pltpu.SemaphoreType.DMA((78,)),
         ],

time: 71.5 us -> 63.6 us (0.89)
  Pallas kernels: 70.7 us -> 62.8 us
    pallas_call x1, Pallas kernels: 68.7 us -> 60.8 us  [network(): pl.pallas_call(net_kernel, out_shape=(jax.ShapeDtypeStruct((ROWS, 128), F...]
where the time goes in v4:
time: 63.6 us; the launch traced here: 63.5 us
  Pallas kernels  62.8 us (99%)
  between operations  0.64 us (1%)
    pallas_call x1, Pallas kernels, network(): pl.pallas_call(net_kernel, out_shape=(jax.ShapeDtypeStruct((ROWS, 128), F...  60.8 us
    pallas_call x1, Pallas kernels, unpack(): pl.pallas_call(unpack_kernel, out_shape=(jax.ShapeDtypeStruct((24, 64), F...  1.99 us

profile of v4, /device:TPU:1, one launch (start us, length us, event | category | flops | bytes accessed | tf_op | source)
XLA Modules:
  0.0 63.5 jit_solution(17232141158210976051)
XLA Ops:
  0.6 60.8 %network.1 = (f32[1536,128]{1,0:T(8,128)}, bf16[8,1024]{1,0:T(8,128)(2,1)}) custom-call(s32[8]{0:T(128)} %bitcast.8, s32[1,1,2,2,8]{4,3,2,1,0:T(2,128)} %bitcast.7, bf16[6,128,256]{2,1,0:T(8,128)(2,1)} %img_hbm.1, f32[8,512]{1,0:T(8,128)} %bitcast.6, f32[8,1024]{1,0:T(8,128)} %bitcast.5, bf16[24,64]{1,0:T(8,128)(2,1)} %w1_hbm.1, bf16[256,128]{1,0:T(8,128)(2,1)} %w2_hbm.1, ...), custom_call_target="tpu_custom_call" | custom-call | tf_op jit(solution)/shard_map/network/pallas_call | solution.py:447
  61.5 2.0 %unpack.1 = (f32[24,64]{1,0:T(8,128)}, f32[256,128]{1,0:T(8,128)}, f32[512,256]{1,0:T(8,128)}, f32[8,256]{1,0:T(8,128)}, bf16[8,1024]{1,0:T(8,128)(2,1)}) custom-call(f32[1536,128]{1,0:T(8,128)} %get-tuple-element.12.full, bf16[8,1024]{1,0:T(8,128)(2,1)} %get-tuple-element.13.shown), custom_call_target="tpu_custom_call" | custom-call | tf_op jit(solution)/shard_map/unpack/pallas_call | solution.py:523

commit v5 on v4

--- a/solution.py
+++ b/solution.py
@@ -129,15 +129,13 @@
 
     pl.semaphore_wait(barrier, len(greeted))
 
-    requests = []
     for k, (dy, dx) in enumerate(DIRECTIONS):
         copy = pltpu.make_async_remote_copy(
             src_ref=msg.at[k], dst_ref=req.at[k],
-            send_sem=req_send.at[k], recv_sem=req_recv.at[k],
+            send_sem=req_send.at[0], recv_sem=req_recv.at[0],
             device_id=device(dy, dx), device_id_type=MESH,
         )
         copy.start()
-        requests.append(copy)
 
     lanes = iota((1024, 128), 1)
     src = iota((1024, 128), 0)
@@ -150,8 +148,8 @@
         place_cut[:, j * 128:(j + 1) * 128] = one_hot(lanes + j * 128 == goal)
 
     fetched[0].wait()
-    for copy in requests:
-        copy.wait()
+    pltpu.make_async_copy(msg, req, req_recv.at[0]).wait()
+    pltpu.make_async_copy(msg, req, req_send.at[0]).wait()
 
     def reply(k):
         dy, dx = step_of(k)
@@ -324,19 +322,14 @@
 
     lax.fori_loop(0, 2, part, 0)
 
-    used = [0]
-
-    def push(src, dst, peer):
-        copy = pltpu.make_async_remote_copy(
-            src_ref=src, dst_ref=dst, send_sem=sum_send.at[used[0]], recv_sem=sum_recv.at[used[0]],
-            device_id=peer, device_id_type=MESH)
-        used[0] += 1
-        copy.start()
-        return copy
-
-    def finish(copies):
-        for copy in copies:
-            copy.wait()
+    def push(at, src, dst, peer):
+        pltpu.make_async_remote_copy(
+            src_ref=src, dst_ref=dst, send_sem=sum_send.at[at], recv_sem=sum_recv.at[at],
+            device_id=peer, device_id_type=MESH).start()
+
+    def finish(at, alike):
+        pltpu.make_async_copy(alike, alike, sum_recv.at[at]).wait()
+        pltpu.make_async_copy(alike, alike, sum_send.at[at]).wait()
 
     def rows(at, count):
         return pl.ds(pl.multiple_of(at, 8), count)
@@ -345,50 +338,51 @@
     far_z = (4, 3, 5, 2, 6, 1, 7)
 
     class Stream:
-        def __init__(self, base, piece, parts, from_core, held_core, from_xy, held_z, from_z):
-            self.base, self.piece, self.half = base, piece, piece * 16
+        def __init__(self, first, base, piece, parts, from_core, held_core, from_xy, held_z, from_z):
+            self.first, self.base, self.piece, self.half = first, base, piece, piece * 16
             self.parts, self.from_core, self.held_core = parts, from_core, held_core
             self.from_xy, self.held_z, self.from_z = from_xy, held_z, from_z
 
         def send_core(self):
-            self.going = [push(self.parts.at[rows((1 - core) * self.half, self.half)], self.from_core, core_peer)]
+            push(self.first, self.parts.at[rows((1 - core) * self.half, self.half)], self.from_core, core_peer)
 
         def send_plane(self):
-            finish(self.going)
+            finish(self.first, self.from_core)
             self.held_core[...] = self.parts[rows(core * self.half, self.half), :] + self.from_core[...]
-            self.going = [
-                push(self.held_core.at[rows(xy_peer(d) * self.piece, self.piece)], self.from_xy.at[d - 1],
-                     place_of(core, xy_peer(d), z)) for d in far_first]
+            for d in far_first:
+                push(self.first + 1, self.held_core.at[rows(xy_peer(d) * self.piece, self.piece)],
+                     self.from_xy.at[d - 1], place_of(core, xy_peer(d), z))
 
         def send_z(self):
-            finish(self.going)
+            finish(self.first + 1, self.from_xy)
             total = self.held_core[rows(xy * self.piece, self.piece), :]
             for d in range(15):
                 total = total + self.from_xy[d]
             self.held_z[...] = total
             self.from_z[z] = total
-            self.going = [push(self.held_z, self.from_z.at[z], z_peer(d)) for d in far_z]
+            for d in far_z:
+                push(self.first + 2, self.held_z, self.from_z.at[z], z_peer(d))
 
         def gather_plane(self):
-            finish(self.going)
+            finish(self.first + 2, self.from_z.at[0:7])
             total = self.from_z[0]
             for d in range(1, 8):
                 total = total + self.from_z[d]
-            at = self.base + core * self.half + xy * self.piece
-            full[rows(at, self.piece), :] = total
-            mine = full.at[rows(at, self.piece)]
-            self.going = [push(mine, mine, place_of(core, xy_peer(d), z)) for d in far_first]
+            mine = full.at[rows(self.base + core * self.half + xy * self.piece, self.piece)]
+            mine[...] = total
+            for d in far_first:
+                push(self.first + 3, mine, mine, place_of(core, xy_peer(d), z))
 
         def gather_core(self):
-            finish(self.going)
+            finish(self.first + 3, self.from_xy)
             mine = full.at[rows(self.base + core * self.half, self.half)]
-            self.going = [push(mine, mine, core_peer)]
+            push(self.first + 4, mine, mine, core_peer)
 
         def end(self):
-            finish(self.going)
-
-    third = Stream(0, 32, parts_a, from_core_a, held_core_a, from_xy_a, held_z_a, from_z_a)
-    others = Stream(1024, 16, parts_b, from_core_b, held_core_b, from_xy_b, held_z_b, from_z_b)
+            finish(self.first + 4, self.from_core)
+
+    third = Stream(0, 0, 32, parts_a, from_core_a, held_core_a, from_xy_a, held_z_a, from_z_a)
+    others = Stream(5, 1024, 16, parts_b, from_core_b, held_core_b, from_xy_b, held_z_b, from_z_b)
 
     take(2)
     pred, delta3 = upward()
@@ -498,8 +492,8 @@
             pltpu.VMEM((8, 16, 128), F32),
             dma, dma, dma, dma, dma,
             pltpu.SemaphoreType.DMA((6,)),
-            pltpu.SemaphoreType.DMA((78,)),
-            pltpu.SemaphoreType.DMA((78,)),
+            pltpu.SemaphoreType.DMA((10,)),
+            pltpu.SemaphoreType.DMA((10,)),
         ],
         compiler_params=pltpu.CompilerParams(
             collective_id=0, has_side_effects=True, vmem_limit_bytes=VMEM_BYTES

time: 63.6 us -> 62.4 us (0.981)
  Pallas kernels: 62.8 us -> 61.6 us
    pallas_call x1, Pallas kernels: 60.8 us -> 59.7 us  [network(): pl.pallas_call(net_kernel, out_shape=(jax.ShapeDtypeStruct((ROWS, 128), F...]
where the time goes in v5:
time: 62.4 us; the launch traced here: 62.3 us
  Pallas kernels  61.6 us (99%)
  between operations  0.64 us (1%)
    pallas_call x1, Pallas kernels, network(): pl.pallas_call(net_kernel, out_shape=(jax.ShapeDtypeStruct((ROWS, 128), F...  59.7 us
    pallas_call x1, Pallas kernels, unpack(): pl.pallas_call(unpack_kernel, out_shape=(jax.ShapeDtypeStruct((24, 64), F...  1.99 us

profile of v5, /device:TPU:1, one launch (start us, length us, event | category | flops | bytes accessed | tf_op | source)
XLA Modules:
  0.0 62.3 jit_solution(5657332014387407999)
XLA Ops:
  0.6 59.7 %network.1 = (f32[1536,128]{1,0:T(8,128)}, bf16[8,1024]{1,0:T(8,128)(2,1)}) custom-call(s32[8]{0:T(128)} %bitcast.8, s32[1,1,2,2,8]{4,3,2,1,0:T(2,128)} %bitcast.7, bf16[6,128,256]{2,1,0:T(8,128)(2,1)} %img_hbm.1, f32[8,512]{1,0:T(8,128)} %bitcast.6, f32[8,1024]{1,0:T(8,128)} %bitcast.5, bf16[24,64]{1,0:T(8,128)(2,1)} %w1_hbm.1, bf16[256,128]{1,0:T(8,128)(2,1)} %w2_hbm.1, ...), custom_call_target="tpu_custom_call" | custom-call | tf_op jit(solution)/shard_map/network/pallas_call | solution.py:441
  60.3 2.0 %unpack.1 = (f32[24,64]{1,0:T(8,128)}, f32[256,128]{1,0:T(8,128)}, f32[512,256]{1,0:T(8,128)}, f32[8,256]{1,0:T(8,128)}, bf16[8,1024]{1,0:T(8,128)(2,1)}) custom-call(f32[1536,128]{1,0:T(8,128)} %get-tuple-element.12.full, bf16[8,1024]{1,0:T(8,128)(2,1)} %get-tuple-element.13.shown), custom_call_target="tpu_custom_call" | custom-call | tf_op jit(solution)/shard_map/unpack/pallas_call | solution.py:517

commit v6 on v5

--- a/solution.py
+++ b/solution.py
@@ -301,12 +301,6 @@
     def part(step, carry):
         @pl.when(step > 0)
         def cutouts():
-            for which in range(2):
-                @pl.when(by_relay[which])
-                def pass_on():
-                    to_relay(which).wait_recv()
-                    onward(which).start()
-
             take(step)
 
         pred, delta3 = upward()
@@ -314,6 +308,12 @@
         @pl.when(step > 0)
         def predictions():
             show(step, pred)
+
+        for which in range(2):
+            @pl.when((step == 0) & by_relay[which])
+            def pass_on():
+                to_relay(which).wait_recv()
+                onward(which).start()
 
         back_third(delta3)
         for ac in range(2):
@@ -334,7 +334,7 @@
     def rows(at, count):
         return pl.ds(pl.multiple_of(at, 8), count)
 
-    far_first = (10, 2, 8, 6, 9, 11, 14, 1, 3, 4, 12, 5, 7, 13, 15)
+    far_first = (10, 6, 9, 14, 11, 2, 8, 5, 15, 7, 13, 1, 4, 3, 12)
     far_z = (4, 3, 5, 2, 6, 1, 7)
 
     class Stream:
@@ -402,9 +402,7 @@
     folded = lax.dot_general(
         one_hot(first_spread(), F32), picked, (((1,), (1,)), ((), ())),
         precision=lax.Precision.HIGHEST, preferred_element_type=F32)
-    parts_b[256:280, :] = lax.dot_general(
-        folded, one_hot((iota((512, 128), 0) & 63) == iota((512, 128), 1), F32), (((1,), (0,)), ((), ())),
-        precision=lax.Precision.HIGHEST, preferred_element_type=F32)
+    parts_b[256:280, :] = folded[:, :128] + folded[:, 128:256] + folded[:, 256:384] + folded[:, 384:]
     parts_b[280:288, :] = gh[:, :128]
     parts_b[288:296, :] = gh[:, 128:]
     parts_b[296:, :] = jnp.zeros((216, 128), F32)
@@ -506,7 +504,8 @@
     o3_ref[:, :128] = full[0:512, :]
     o3_ref[:, 128:] = full[512:1024, :]
     o2_ref[...] = full[1024:1280, :]
-    o1_ref[...] = full[1280:1304, :64]
+    first = full[1280:1304, :]
+    o1_ref[...] = first[:, :64] + first[:, 64:]
     oh_ref[:, :128] = full[1304:1312, :]
     oh_ref[:, 128:] = full[1312:1320, :]
     cut_pred_ref[...] = shown[...]

time: 62.4 us -> 61.3 us (0.982)
  Pallas kernels: 61.6 us -> 60.6 us
    pallas_call x1, Pallas kernels: 59.7 us -> 58.6 us  [network(): pl.pallas_call(net_kernel, out_shape=(jax.ShapeDtypeStruct((ROWS, 128), F...]
where the time goes in v6:
time: 61.3 us; the launch traced here: 61.2 us
  Pallas kernels  60.6 us (99%)
  between operations  0.64 us (1%)
    pallas_call x1, Pallas kernels, network(): pl.pallas_call(net_kernel, out_shape=(jax.ShapeDtypeStruct((ROWS, 128), F...  58.6 us
    pallas_call x1, Pallas kernels, unpack(): pl.pallas_call(unpack_kernel, out_shape=(jax.ShapeDtypeStruct((24, 64), F...  1.99 us

profile of v6, /device:TPU:1, one launch (start us, length us, event | category | flops | bytes accessed | tf_op | source)
XLA Modules:
  0.0 61.2 jit_solution(12127216342407579819)
XLA Ops:
  0.6 58.6 %network.1 = (f32[1536,128]{1,0:T(8,128)}, bf16[8,1024]{1,0:T(8,128)(2,1)}) custom-call(s32[8]{0:T(128)} %bitcast.8, s32[1,1,2,2,8]{4,3,2,1,0:T(2,128)} %bitcast.7, bf16[6,128,256]{2,1,0:T(8,128)(2,1)} %img_hbm.1, f32[8,512]{1,0:T(8,128)} %bitcast.6, f32[8,1024]{1,0:T(8,128)} %bitcast.5, bf16[24,64]{1,0:T(8,128)(2,1)} %w1_hbm.1, bf16[256,128]{1,0:T(8,128)(2,1)} %w2_hbm.1, ...), custom_call_target="tpu_custom_call" | custom-call | tf_op jit(solution)/shard_map/network/pallas_call | solution.py:439
  59.2 2.0 %unpack.1 = (f32[24,64]{1,0:T(8,128)}, f32[256,128]{1,0:T(8,128)}, f32[512,256]{1,0:T(8,128)}, f32[8,256]{1,0:T(8,128)}, bf16[8,1024]{1,0:T(8,128)(2,1)}) custom-call(f32[1536,128]{1,0:T(8,128)} %get-tuple-element.12.full, bf16[8,1024]{1,0:T(8,128)(2,1)} %get-tuple-element.13.shown), custom_call_target="tpu_custom_call" | custom-call | tf_op jit(solution)/shard_map/unpack/pallas_call | solution.py:516

commit v7 on v6

--- a/solution.py
+++ b/solution.py
@@ -438,7 +438,7 @@
     dma = pltpu.SemaphoreType.DMA((8,))
     return pl.pallas_call(
         net_kernel,
-        out_shape=(jax.ShapeDtypeStruct((ROWS, 128), F32), jax.ShapeDtypeStruct((8, 1024), BF)),
+        out_shape=(pltpu.VMEM((ROWS, 128), F32), pltpu.VMEM((8, 1024), BF)),
         in_specs=[pl.BlockSpec(memory_space=pltpu.SMEM), vmem] + [pl.BlockSpec(memory_space=pl.ANY)] * 7,
         out_specs=(vmem, vmem),
         scratch_shapes=[
@@ -525,7 +525,7 @@
         in_specs=[vmem, vmem],
         out_specs=(vmem,) * 5,
         name="unpack",
-    )(full, shown)
+    )(pltpu.with_memory_space_constraint(full, pltpu.VMEM), pltpu.with_memory_space_constraint(shown, pltpu.VMEM))
 
 
 def per_device(sky_tile, request_offset, request_count, tile_target, cut_target, w_first, w_second, w_third, w_head):

time: 61.3 us -> 59.2 us (0.966)
  Pallas kernels: 60.6 us -> 58.5 us
    pallas_call x1, Pallas kernels: 1.99 us -> 0.85 us  [unpack(): pl.pallas_call(unpack_kernel, out_shape=(jax.ShapeDtypeStruct((24, 64), F...]
    pallas_call x1, Pallas kernels: 58.6 us -> 57.6 us  [network(): pl.pallas_call(net_kernel, out_shape=(pltpu.VMEM((ROWS, 128), F32), pltpu...]
where the time goes in v7:
time: 59.2 us; the launch traced here: 59.1 us
  Pallas kernels  58.5 us (99%)
  between operations  0.64 us (1%)
    pallas_call x1, Pallas kernels, network(): pl.pallas_call(net_kernel, out_shape=(pltpu.VMEM((ROWS, 128), F32), pltpu...  57.6 us

profile of v7, /device:TPU:1, one launch (start us, length us, event | category | flops | bytes accessed | tf_op | source)
XLA Modules:
  0.0 59.1 jit_solution(15473315283680189444)
XLA Ops:
  0.6 57.6 %network.1 = (f32[1536,128]{1,0:T(8,128)S(1)}, bf16[8,1024]{1,0:T(8,128)(2,1)S(1)}) custom-call(s32[8]{0:T(128)} %bitcast.8, s32[1,1,2,2,8]{4,3,2,1,0:T(2,128)} %bitcast.7, bf16[6,128,256]{2,1,0:T(8,128)(2,1)} %img_hbm.1, f32[8,512]{1,0:T(8,128)} %bitcast.6, f32[8,1024]{1,0:T(8,128)} %bitcast.5, bf16[24,64]{1,0:T(8,128)(2,1)} %w1_hbm.1, ...), custom_call_target="tpu_custom_call" | custom-call | tf_op jit(solution)/shard_map/network/pallas_call | solution.py:439
  58.3 0.9 %unpack.1 = (f32[24,64]{1,0:T(8,128)}, f32[256,128]{1,0:T(8,128)}, f32[512,256]{1,0:T(8,128)}, f32[8,256]{1,0:T(8,128)}, bf16[8,1024]{1,0:T(8,128)(2,1)}) custom-call(f32[1536,128]{1,0:T(8,128)S(1)} %get-tuple-element.12.full, bf16[8,1024]{1,0:T(8,128)(2,1)S(1)} %get-tuple-element.13.shown), custom_call_target="tpu_custom_call" | custom-call | tf_op jit(solution)/shard_map/unpack/pallas_call | solution.py:516
